TPU v7x, 32 devices: a whole 2x2x4 slice. The times are simulated.
32 devices in a mesh: section: 4 (over y, x), dp: 8 (over z, core).
Axes of the slice: x: 2, y: 2, z: 4, core: 2. Of those that a mesh axis runs over, the one named last changes fastest.
Arguments:
- enter_a: bfloat16 [4, 1024, 7168], P('section', 'dp'), may hold values from -6 to 6
- enter_b: bfloat16 [4, 1024, 7168], P('section', 'dp'), may hold values from -6 to 6
- cotan_a: bfloat16 [4, 1024, 7168], P('section', 'dp'), may hold values from -6 to 6
- cotan_b: bfloat16 [4, 1024, 7168], P('section', 'dp'), may hold values from -6 to 6
- saved_a: bfloat16 [2, 4, 1024, 7168], P(None, 'section', 'dp'), may hold values from -6 to 6
- saved_b: bfloat16 [2, 4, 1024, 7168], P(None, 'section', 'dp'), may hold values from -6 to 6
- norm_gain: float32 [4, 7168], P('section'), may hold values from 0.1 to 1.9
- w_down: bfloat16 [4, 7168, 256], P('section', 'dp'), may hold values from -0.0625 to 0.0625
- latent_gain: float32 [4, 256], P('section'), may hold values from 0.1 to 1.9
- w_up: bfloat16 [4, 256, 7168], P('section', None, 'dp'), may hold values from -0.375 to 0.375
Outputs:
- out_a: bfloat16 [4, 1024, 7168], P('section', 'dp')
- out_b: bfloat16 [4, 1024, 7168], P('section', 'dp')
- back_a: bfloat16 [4, 1024, 7168], P('section', 'dp')
- back_b: bfloat16 [4, 1024, 7168], P('section', 'dp')
- grad_norm_gain: float32 [4, 7168], P('section', 'dp')
- grad_down: float32 [4, 7168, 256], P('section', 'dp')
- grad_latent_gain: float32 [4, 256], P('section', 'dp')
- grad_up: float32 [4, 256, 7168], P('section', None, 'dp')
All inputs are finite; a program needn't handle non-finite values.
Results may differ from a plain program's by a relative error of at most 0.035.
Values may be sent and summed in bfloat16 or wider, within the bound.
A program may use at most 192 MiB of HBM per device.

v0:
```python
import jax
import jax.numpy as jnp
from jax import lax
from jax.sharding import PartitionSpec as P

TICKS = 2


def swapped(value, axis, distance):
    return lax.ppermute(value, axis, [(i, i ^ 1 << distance) for i in range(lax.axis_size(axis))])


def from_behind(block, axis, distance):
    devices = range(lax.axis_size(axis))
    route = [(i - distance, i) for i in devices if i - distance in devices]
    return lax.ppermute(block, axis, route)


def shortened(value):

    def short(part):
        return part.astype(jnp.bfloat16) if part.dtype == jnp.float32 else part

    return jax.tree.map(short, value)


def layer(x, norm_gain, w_down, latent_gain, w_up):
    xf = x.astype(jnp.float32)
    normed = (xf * lax.rsqrt(jnp.mean(xf * xf, axis=-1, keepdims=True) + 1e-06) * norm_gain).astype(
        jnp.bfloat16
    )
    latent = jnp.dot(normed, w_down, preferred_element_type=jnp.float32)
    scaled = (
        latent * lax.rsqrt(jnp.mean(latent * latent, axis=-1, keepdims=True) + 1e-06) * latent_gain
    ).astype(jnp.bfloat16)
    return (xf + jnp.dot(scaled, w_up, preferred_element_type=jnp.float32)).astype(jnp.bfloat16)


def layer_grads(x, cotangent, weights):
    _, pull = jax.vjp(layer, x, *weights)
    return pull(cotangent)


def body(
    enter_a, enter_b, cotan_a, cotan_b, saved_a, saved_b, norm_gain, w_down, latent_gain, w_up
):
    section_count = lax.axis_size("section")
    section_bits = section_count.bit_length() - 1
    moved = (norm_gain, w_down, latent_gain, w_up)
    for bit in range(section_bits):
        moved = (
            swapped(moved[0].astype(jnp.bfloat16), "section", bit).astype(jnp.float32),
            swapped(moved[1], "section", bit),
            swapped(moved[2].astype(jnp.bfloat16), "section", bit).astype(jnp.float32),
            swapped(moved[3], "section", bit),
        )
    mirror_small = tuple((v[0] for v in moved))
    full = (
        lax.all_gather(w_down[0], "dp", axis=0, tiled=True),
        lax.all_gather(w_up[0], "dp", axis=1, tiled=True),
        lax.all_gather(mirror_small[1], "dp", axis=0, tiled=True),
        lax.all_gather(mirror_small[3], "dp", axis=1, tiled=True),
    )
    own_weights = (norm_gain[0], full[0], latent_gain[0], full[1])
    mirror_weights = (mirror_small[0], full[2], mirror_small[2], full[3])
    accum_own = tuple((jnp.zeros(v.shape, jnp.float32) for v in own_weights))
    accum_mirror = tuple((jnp.zeros(v.shape, jnp.float32) for v in mirror_weights))
    state_a = enter_a[0]
    state_b = enter_b[0]
    grad_a = cotan_a[0]
    grad_b = cotan_b[0]
    for tick in range(TICKS):
        out_a = layer(state_a, *own_weights)
        out_b = layer(state_b, *mirror_weights)
        result_a = layer_grads(saved_a[tick, 0], grad_a, own_weights)
        result_b = layer_grads(saved_b[tick, 0], grad_b, mirror_weights)
        back_a = result_a[0]
        back_b = result_b[0]
        accum_own = tuple((p + q.astype(jnp.float32) for p, q in zip(accum_own, result_a[1:])))
        accum_mirror = tuple(
            (p + q.astype(jnp.float32) for p, q in zip(accum_mirror, result_b[1:]))
        )
        if tick < TICKS - 1:
            state_a = from_behind(out_a, "section", 1)
            state_b = from_behind(out_b, "section", -1)
            grad_a = from_behind(back_a, "section", -1)
            grad_b = from_behind(back_b, "section", 1)
    part_own = tuple((v.astype(jnp.bfloat16) for v in accum_own))
    part_mirror = tuple((v.astype(jnp.bfloat16) for v in accum_mirror))
    paired = tuple((jnp.stack([p, q]) for p, q in zip(part_own, part_mirror)))
    sums = (
        lax.psum_scatter(paired[0], "dp", scatter_dimension=1, tiled=True).astype(jnp.float32),
        lax.psum_scatter(paired[1], "dp", scatter_dimension=1, tiled=True).astype(jnp.float32),
        lax.psum_scatter(paired[2], "dp", scatter_dimension=1, tiled=True).astype(jnp.float32),
        lax.psum_scatter(paired[3], "dp", scatter_dimension=2, tiled=True).astype(jnp.float32),
    )
    mine = tuple((v[0] for v in sums))
    theirs = tuple((v[1] for v in sums))
    arrived = theirs
    for bit in range(section_bits):
        arrived = swapped(
            (
                shortened(arrived[0]),
                shortened(arrived[1]),
                shortened(arrived[2]),
                shortened(arrived[3]),
            ),
            "section",
            bit,
        )
    totals = tuple((p + q for p, q in zip(mine, arrived)))
    return (
        out_a[None],
        out_b[None],
        back_a[None],
        back_b[None],
        totals[0][None],
        totals[1][None],
        totals[2][None],
        totals[3][None],
    )


def solution(mesh):
    placed = (
        P("section", "dp", None),
        P("section", "dp", None),
        P("section", "dp", None),
        P("section", "dp", None),
        P(None, "section", "dp", None),
        P(None, "section", "dp", None),
        P("section", None),
        P("section", "dp", None),
        P("section", None),
        P("section", None, "dp"),
    )
    return jax.shard_map(
        body,
        mesh=mesh,
        in_specs=placed,
        out_specs=(
            P("section", "dp", None),
            P("section", "dp", None),
            P("section", "dp", None),
            P("section", "dp", None),
            P("section", "dp"),
            P("section", "dp", None),
            P("section", "dp"),
            P("section", None, "dp"),
        ),
        check_vma=False,
    )
```

profile of v0, /device:TPU:0, one launch (start us, length us, event | category | flops | bytes accessed | tf_op | source)
XLA Modules:
  0.0 501.3 jit_solution(15608009872207780699)
XLA Ops:
  11.7 10.7 %collective-permute-done.3 = bf16[1,896,256]{2,1,0:T(8,128)(2,1)S(1)} collective-permute-done((bf16[1,896,256]{2,1,0:T(8,128)(2,1)}, bf16[1,896,256]{2,1,0:T(8,128)(2,1)S(1)}, u32[]{:S(2)}, u32[]{:S(2)}) %collective-permute-start.3) | collective-permute-done | bytes 458784 | tf_op jit(solution)/shard_map/ppermute | solution.py:10
  24.2 9.9 %collective-permute-done.4 = bf16[1,896,256]{2,1,0:T(8,128)(2,1)S(1)} collective-permute-done((bf16[1,896,256]{2,1,0:T(8,128)(2,1)S(1)}, bf16[1,896,256]{2,1,0:T(8,128)(2,1)S(1)}, u32[]{:S(2)}, u32[]{:S(2)}) %collective-permute-start.4) | collective-permute-done | bytes 458784 | tf_op jit(solution)/shard_map/ppermute | solution.py:10
  36.5 9.7 %collective-permute-done.7 = bf16[1,256,896]{2,1,0:T(8,128)(2,1)S(1)} collective-permute-done((bf16[1,256,896]{2,1,0:T(8,128)(2,1)}, bf16[1,256,896]{2,1,0:T(8,128)(2,1)S(1)}, u32[]{:S(2)}, u32[]{:S(2)}) %collective-permute-start.7) | collective-permute-done | bytes 458784 | tf_op jit(solution)/shard_map/ppermute | solution.py:10
  47.3 8.9 %collective-permute-done.8 = bf16[1,256,896]{2,1,0:T(8,128)(2,1)S(1)} collective-permute-done((bf16[1,256,896]{2,1,0:T(8,128)(2,1)S(1)}, bf16[1,256,896]{2,1,0:T(8,128)(2,1)S(1)}, u32[]{:S(2)}, u32[]{:S(2)}) %collective-permute-start.8) | collective-permute-done | bytes 458784 | tf_op jit(solution)/shard_map/ppermute | solution.py:10
  69.5 3.5 multiply_reduce_fusion.11
  73.0 25.2 %all-gather.11.cloned.1.call-done = bf16[1,256,7168]{2,1,0:T(8,128)(2,1)} async-done(((bf16[1,256,896]{2,1,0:T(8,128)(2,1)}), bf16[1,256,7168]{2,1,0:T(8,128)(2,1)}) %all-gather.11.cloned.1.call-update) | async-done | bytes 3670032 | tf_op jit(solution)/shard_map/all_gather | solution.py:60
  98.2 3.6 multiply_reduce_fusion.3
  101.9 3.8 fusion.45
  110.2 31.7 %all-gather.13.cloned.1.call-done = bf16[1,7168,256]{2,1,0:T(8,128)(2,1)} async-done(((bf16[1,896,256]{2,1,0:T(8,128)(2,1)}), bf16[1,7168,256]{2,1,0:T(8,128)(2,1)}) %all-gather.13.cloned.1.call-update) | async-done | bytes 3670032 | tf_op jit(solution)/shard_map/all_gather | solution.py:61
  141.9 3.4 multiply_reduce_fusion.7
  145.3 40.3 %all-gather.15.cloned.1.call-done = bf16[1,256,7168]{2,1,0:T(8,128)(2,1)} async-done(((bf16[1,256,896]{2,1,0:T(8,128)(2,1)}), bf16[1,256,7168]{2,1,0:T(8,128)(2,1)}) %all-gather.15.cloned.1.call-update) | async-done | bytes 3670032 | tf_op jit(solution)/shard_map/all_gather | solution.py:62
  185.5 4.2 multiply_reduce_fusion.1
  189.8 3.9 fusion.41
  194.9 3.7 collective-permute-start.11
  205.0 3.3 fusion.19
  208.3 29.7 %collective-permute-done.11 = bf16[128,7168]{1,0:T(8,128)(2,1)S(1)} collective-permute-done((bf16[128,7168]{1,0:T(8,128)(2,1)S(1)}, bf16[128,7168]{1,0:T(8,128)(2,1)S(1)}, u32[]{:S(2)}, u32[]{:S(2)}) %collective-permute-start.11) | collective-permute-done | bytes 1835040 | tf_op jit(solution)/shard_map/ppermute | solution.py:16
  240.6 3.3 fusion.18
  244.8 6.8 %pad_maximum_fusion = bf16[2,7168,256]{2,1,0:T(8,128)(2,1)} fusion(bf16[1,7168,256]{2,1,0:T(8,128)(2,1)} %fusion.18, bf16[1,7168,256]{2,1,0:T(8,128)(2,1)} %fusion.19), kind=kLoop, calls=%fused_computation.46 | loop fusion | flops 3670016 | bytes 14680064 | tf_op jit(solution)/shard_map/stack | solution.py:90
  258.8 3.7 pad_maximum_fusion.1
  262.5 18.6 %copy.22 = bf16[2,256,7168]{1,0,2:T(2,128)(2,1)} copy(bf16[2,256,7168]{2,1,0:T(8,128)(2,1)} %pad_maximum_fusion.1) | data formatting | bytes 14680064
  281.1 7.6 %copy.31 = bf16[896,8,2,256]{3,1,2,0:T(8,128)(2,1)} copy(bf16[896,8,2,256]{3,2,1,0:T(2,128)(2,1)} %bitcast.234) | data formatting | bytes 14680064
  292.8 3.1 multiply_reduce_fusion.15
  296.8 4.6 collective-permute-start
  307.9 32.4 %collective-permute-done = bf16[128,7168]{1,0:T(8,128)(2,1)S(1)} collective-permute-done((bf16[128,7168]{1,0:T(8,128)(2,1)S(1)}, bf16[128,7168]{1,0:T(8,128)(2,1)S(1)}, u32[]{:S(2)}, u32[]{:S(2)}) %collective-permute-start) | collective-permute-done | bytes 1835040 | tf_op jit(solution)/shard_map/ppermute | solution.py:16
  341.6 4.0 fusion.105
  348.3 3.5 fusion.39
  353.9 28.4 %collective-permute-done.9 = bf16[128,7168]{1,0:T(8,128)(2,1)} collective-permute-done((bf16[128,7168]{1,0:T(8,128)(2,1)}, bf16[128,7168]{1,0:T(8,128)(2,1)}, u32[]{:S(2)}, u32[]{:S(2)}) %collective-permute-start.9) | collective-permute-done | bytes 1835040 | tf_op jit(solution)/shard_map/ppermute | solution.py:16
  384.3 3.4 multiply_reduce_fusion.12
  387.8 4.8 fusion.28
  402.3 33.1 %reduce-scatter.17.cloned.1.call-done = bf16[896,512]{1,0:T(8,128)(2,1)} async-done(((bf16[7168,512]{1,0:T(8,128)(2,1)}), bf16[896,512]{1,0:T(8,128)(2,1)}) %reduce-scatter.17.cloned.1.call-update) | async-done | bytes 917520
  443.0 28.4 %reduce-scatter.13.cloned.1.call-done = bf16[896,2]{1,0:T(8,128)(2,1)} async-done(((bf16[7168,2]{1,0:T(8,128)(2,1)}), bf16[896,2]{1,0:T(8,128)(2,1)}) %reduce-scatter.13.cloned.1.call-update) | async-done | bytes 3600
  478.5 9.5 %collective-permute-done.13 = bf16[896]{0:T(1024)(128)(2,1)S(1)} collective-permute-done((bf16[896]{0:T(1024)(128)(2,1)S(1)}, bf16[896]{0:T(1024)(128)(2,1)S(1)}, u32[]{:S(2)}, u32[]{:S(2)}) %collective-permute-start.13) | collective-permute-done | bytes 1824 | tf_op jit(solution)/shard_map/ppermute | solution.py:10
  (182 shorter events, 95.4 us)
Async XLA Ops:
  7.2 62.3 %copy-start.18 = (f32[1,7168]{1,0:T(1,128)S(1)}, f32[1,7168]{1,0:T(1,128)}, u32[]{:S(2)}) copy-start(f32[1,7168]{1,0:T(1,128)} %param.16) | copy-start | bytes 86020
  7.2 62.2 %all-gather.9.cloned.1.call-start = ((), (), s32[]{:S(2)}) async-start(), calls=%async_computation.5 | async-start | bytes 4128768 | tf_op jit(solution)/shard_map/all_gather | solution.py:59
  7.9 90.3 %all-gather.11.cloned.1.call-start = ((), (), s32[]{:S(2)}) async-start(), calls=%async_computation.6 | async-start | bytes 4128768 | tf_op jit(solution)/shard_map/all_gather | solution.py:60
  8.7 133.2 %all-gather.13.cloned.1.call-start = ((), (), s32[]{:S(2)}) async-start(), calls=%async_computation.7 | async-start | bytes 4128768 | tf_op jit(solution)/shard_map/all_gather | solution.py:61
  8.7 13.7 %collective-permute-start.3 = (bf16[1,896,256]{2,1,0:T(8,128)(2,1)}, bf16[1,896,256]{2,1,0:T(8,128)(2,1)S(1)}, u32[]{:S(2)}, u32[]{:S(2)}) collective-permute-start(bf16[1,896,256]{2,1,0:T(8,128)(2,1)} %param.17), channel_id=1, source_target_pairs={{0,8},{8,0},{16,24},{24,16},{1,9},{9,1},{17,25},{25,17},{2,10},{10... | collective-permute-start | bytes 1376264 | tf_op jit(solution)/shard_map/ppermute | solution.py:10
  22.4 11.7 %collective-permute-start.4 = (bf16[1,896,256]{2,1,0:T(8,128)(2,1)S(1)}, bf16[1,896,256]{2,1,0:T(8,128)(2,1)S(1)}, u32[]{:S(2)}, u32[]{:S(2)}) collective-permute-start(bf16[1,896,256]{2,1,0:T(8,128)(2,1)S(1)} %collective-permute-done.3), channel_id=1, source_target_pairs={{0,16},{8,24},{16,0},{24,8},{1,17},{9,25},{17,1},{25,9},{2,18},{10... | collective-permute-start | bytes 1376264 | tf_op jit(solution)/shard_map/ppermute | solution.py:10
  34.9 150.6 %all-gather.15.cloned.1.call-start = ((), (), s32[]{:S(2)}) async-start(), calls=%async_computation.8 | async-start | bytes 4128768 | tf_op jit(solution)/shard_map/all_gather | solution.py:62
  35.0 11.2 %collective-permute-start.7 = (bf16[1,256,896]{2,1,0:T(8,128)(2,1)}, bf16[1,256,896]{2,1,0:T(8,128)(2,1)S(1)}, u32[]{:S(2)}, u32[]{:S(2)}) collective-permute-start(bf16[1,256,896]{2,1,0:T(8,128)(2,1)} %param.19), channel_id=1, source_target_pairs={{0,8},{8,0},{16,24},{24,16},{1,9},{9,1},{17,25},{25,17},{2,10},{10... | collective-permute-start | bytes 1376264 | tf_op jit(solution)/shard_map/ppermute | solution.py:10
  46.1 10.1 %collective-permute-start.8 = (bf16[1,256,896]{2,1,0:T(8,128)(2,1)S(1)}, bf16[1,256,896]{2,1,0:T(8,128)(2,1)S(1)}, u32[]{:S(2)}, u32[]{:S(2)}) collective-permute-start(bf16[1,256,896]{2,1,0:T(8,128)(2,1)S(1)} %collective-permute-done.7), channel_id=1, source_target_pairs={{0,16},{8,24},{16,0},{24,8},{1,17},{9,25},{17,1},{25,9},{2,18},{10... | collective-permute-start | bytes 1376264 | tf_op jit(solution)/shard_map/ppermute | solution.py:10
  57.0 338.9 %reduce-scatter.15.cloned.1.call-start = ((), (), s32[]{:S(2)}) async-start(), calls=%async_computation.10 | async-start | bytes 73728
  57.8 7.7 %collective-permute-start.1 = (bf16[1,7168]{1,0:T(2,128)(2,1)S(1)}, bf16[1,7168]{1,0:T(2,128)(2,1)S(1)}, u32[]{:S(2)}, u32[]{:S(2)}) collective-permute-start(bf16[1,7168]{1,0:T(2,128)(2,1)S(1)} %convert_element_type.341), channel_id=1, source_target_pairs={{0,8},{8,0},{16,24},{24,16},{1,9},{9,1},{17,25},{25,17},{2,10},{10... | collective-permute-start | bytes 43016 | tf_op jit(solution)/shard_map/ppermute | solution.py:10
  59.4 5.2 %collective-permute-start.5 = (bf16[1,256]{1,0:T(2,128)(2,1)S(1)}, bf16[1,256]{1,0:T(2,128)(2,1)S(1)}, u32[]{:S(2)}, u32[]{:S(2)}) collective-permute-start(bf16[1,256]{1,0:T(2,128)(2,1)S(1)} %convert_element_type.343), channel_id=1, source_target_pairs={{0,8},{8,0},{16,24},{24,16},{1,9},{9,1},{17,25},{25,17},{2,10},{10... | collective-permute-start | bytes 1544 | tf_op jit(solution)/shard_map/ppermute | solution.py:10
  64.6 3.6 collective-permute-start.6
  65.5 3.9 collective-permute-start.2
  69.4 28.8 %copy-start.10 = (bf16[1,128,7168]{2,1,0:T(8,128)(2,1)S(1)}, bf16[1,128,7168]{2,1,0:T(8,128)(2,1)}, u32[]{:S(2)}) copy-start(bf16[1,128,7168]{2,1,0:T(8,128)(2,1)} %param.12) | copy-start | bytes 5505028
  69.4 28.8 %copy-start.21 = (f32[1,256]{1,0:T(1,128)S(1)}, f32[1,256]{1,0:T(1,128)}, u32[]{:S(2)}) copy-start(f32[1,256]{1,0:T(1,128)} %param.18) | copy-start | bytes 3076
  108.1 91.3 %collective-permute-start.10 = (bf16[128,7168]{1,0:T(8,128)(2,1)}, bf16[128,7168]{1,0:T(8,128)(2,1)}, u32[]{:S(2)}, u32[]{:S(2)}) collective-permute-start(bf16[128,7168]{1,0:T(8,128)(2,1)} %fusion.52), channel_id=1, source_target_pairs={{8,0},{16,8},{24,16},{9,1},{17,9},{25,17},{10,2},{18,10},{26,18},{... | collective-permute-start | bytes 5505032 | tf_op jit(solution)/shard_map/ppermute | solution.py:16
  194.9 43.0 %collective-permute-start.11 = (bf16[128,7168]{1,0:T(8,128)(2,1)S(1)}, bf16[128,7168]{1,0:T(8,128)(2,1)S(1)}, u32[]{:S(2)}, u32[]{:S(2)}) collective-permute-start(bf16[128,7168]{1,0:T(8,128)(2,1)S(1)} %fusion.54), channel_id=1, source_target_pairs={{0,8},{8,16},{16,24},{1,9},{9,17},{17,25},{2,10},{10,18},{18,26},{... | collective-permute-start | bytes 5505032 | tf_op jit(solution)/shard_map/ppermute | solution.py:16
  205.0 33.0 %copy-start.2 = (bf16[1,256,7168]{2,1,0:T(8,128)(2,1)S(1)}, bf16[1,256,7168]{2,1,0:T(8,128)(2,1)}, u32[]{:S(2)}) copy-start(bf16[1,256,7168]{2,1,0:T(8,128)(2,1)} %all-gather.15.cloned.1.call-done) | copy-start | bytes 11010052
  244.7 155.6 %reduce-scatter.11.cloned.1.call-start = ((), (), s32[]{:S(2)}) async-start(), calls=%async_computation.4 | async-start | bytes 8257536 | tf_op jit(solution)/shard_map/reduce_scatter | solution.py:93
  251.6 183.8 %reduce-scatter.17.cloned.1.call-start = ((), (), s32[]{:S(2)}) async-start(), calls=%async_computation.11 | async-start | bytes 8257536
  288.7 182.6 %reduce-scatter.13.cloned.1.call-start = ((), (), s32[]{:S(2)}) async-start(), calls=%async_computation.9 | async-start | bytes 2064384
  296.8 43.5 %collective-permute-start = (bf16[128,7168]{1,0:T(8,128)(2,1)S(1)}, bf16[128,7168]{1,0:T(8,128)(2,1)S(1)}, u32[]{:S(2)}, u32[]{:S(2)}) collective-permute-start(bf16[128,7168]{1,0:T(8,128)(2,1)S(1)} %fusion.20), channel_id=1, source_target_pairs={{0,8},{8,16},{16,24},{1,9},{9,17},{17,25},{2,10},{10,18},{18,26},{... | collective-permute-start | bytes 5505032 | tf_op jit(solution)/shard_map/ppermute | solution.py:16
  304.2 78.2 %collective-permute-start.9 = (bf16[128,7168]{1,0:T(8,128)(2,1)}, bf16[128,7168]{1,0:T(8,128)(2,1)}, u32[]{:S(2)}, u32[]{:S(2)}) collective-permute-start(bf16[128,7168]{1,0:T(8,128)(2,1)} %fusion.22), channel_id=1, source_target_pairs={{8,0},{16,8},{24,16},{9,1},{17,9},{25,17},{10,2},{18,10},{26,18},{... | collective-permute-start | bytes 5505032 | tf_op jit(solution)/shard_map/ppermute | solution.py:16
  396.8 3.5 collective-permute-start.16
  400.4 75.3 %collective-permute-start.17 = (bf16[32]{0:T(256)(128)(2,1)S(1)}, bf16[32]{0:T(256)(128)(2,1)S(1)}, u32[]{:S(2)}, u32[]{:S(2)}) collective-permute-start(bf16[32]{0:T(256)(128)(2,1)S(1)} %collective-permute-done.16), channel_id=1, source_target_pairs={{0,16},{8,24},{16,0},{24,8},{1,17},{9,25},{17,1},{25,9},{2,18},{10... | collective-permute-start | bytes 200 | tf_op jit(solution)/shard_map/ppermute | solution.py:10
  401.4 72.9 %collective-permute-start.14 = (bf16[896,256]{1,0:T(8,128)(2,1)S(1)}, bf16[896,256]{1,0:T(8,128)(2,1)}, u32[]{:S(2)}, u32[]{:S(2)}) collective-permute-start(bf16[896,256]{1,0:T(8,128)(2,1)S(1)} %slice_bitcast_fusion), channel_id=1, source_target_pairs={{0,8},{8,0},{16,24},{24,16},{1,9},{9,1},{17,25},{25,17},{2,10},{10... | collective-permute-start | bytes 1376264 | tf_op jit(solution)/shard_map/ppermute | solution.py:10
  441.5 36.3 %collective-permute-start.18 = (bf16[256,896]{1,0:T(8,128)(2,1)}, bf16[256,896]{1,0:T(8,128)(2,1)S(1)}, u32[]{:S(2)}, u32[]{:S(2)}) collective-permute-start(bf16[256,896]{1,0:T(8,128)(2,1)} %bitcast.37), channel_id=1, source_target_pairs={{0,8},{8,0},{16,24},{24,16},{1,9},{9,1},{17,25},{25,17},{2,10},{10... | collective-permute-start | bytes 1376264 | tf_op jit(solution)/shard_map/ppermute | solution.py:10
  472.6 3.7 collective-permute-start.12
  474.3 15.8 %collective-permute-start.15 = (bf16[896,256]{1,0:T(8,128)(2,1)}, bf16[896,256]{1,0:T(8,128)(2,1)S(1)}, u32[]{:S(2)}, u32[]{:S(2)}) collective-permute-start(bf16[896,256]{1,0:T(8,128)(2,1)} %collective-permute-done.14), channel_id=1, source_target_pairs={{0,16},{8,24},{16,0},{24,8},{1,17},{9,25},{17,1},{25,9},{2,18},{10... | collective-permute-start | bytes 1376264 | tf_op jit(solution)/shard_map/ppermute | solution.py:10
  476.3 11.7 %collective-permute-start.13 = (bf16[896]{0:T(1024)(128)(2,1)S(1)}, bf16[896]{0:T(1024)(128)(2,1)S(1)}, u32[]{:S(2)}, u32[]{:S(2)}) collective-permute-start(bf16[896]{0:T(1024)(128)(2,1)S(1)} %collective-permute-done.12), channel_id=1, source_target_pairs={{0,16},{8,24},{16,0},{24,8},{1,17},{9,25},{17,1},{25,9},{2,18},{10... | collective-permute-start | bytes 5384 | tf_op jit(solution)/shard_map/ppermute | solution.py:10
  477.8 15.1 %collective-permute-start.19 = (bf16[256,896]{1,0:T(8,128)(2,1)S(1)}, bf16[256,896]{1,0:T(8,128)(2,1)S(1)}, u32[]{:S(2)}, u32[]{:S(2)}) collective-permute-start(bf16[256,896]{1,0:T(8,128)(2,1)S(1)} %collective-permute-done.18), channel_id=1, source_target_pairs={{0,16},{8,24},{16,0},{24,8},{1,17},{9,25},{17,1},{25,9},{2,18},{10... | collective-permute-start | bytes 1376264 | tf_op jit(solution)/shard_map/ppermute | solution.py:10
  (22 other events, 79.7 us)
Sparse Core Ops, SparseCore 0:
  9.7 45.2 all-gather.8
  56.6 41.5 all-gather.10
  100.4 41.4 all-gather.12
  143.9 41.5 all-gather.14
  244.9 29.8 reduce-scatter.14
  277.0 77.8 reduce-scatter.10
  357.3 78.0 reduce-scatter.16
  437.8 33.4 reduce-scatter.12
where the time goes:
time: 510 us; the launch traced here: 501 us
  waiting for transfers between devices  306 us (60%)
  matrix products  66.8 us (13%)
  local copies, waits for them, and re-layouts  45.7 us (9%)
  other arithmetic  36.3 us (7%)
  starting transfers between devices  31.8 us (6%)
  between operations  15.2 us (3%)
    ppermute x4, waiting for transfers between devices, from_behind(): return lax.ppermute(block, axis, route)  90.5 us
    unnamed x11, waiting for transfers between devices  63 us
    ppermute x16, waiting for transfers between devices, swapped(): lax.ppermute(value, axis, [(i, i ^ 1 << distance) for i in range(lax.axis...  54.8 us
    unnamed x62, local copies, waits for them, and re-layouts  40.6 us
    all_gather x1, waiting for transfers between devices, body(): lax.all_gather(mirror_small[3], 'dp', axis=1, tiled=True)  40.3 us
    dot_general x16, matrix products, layer(): latent = jnp.dot(normed, w_down, preferred_element_type=jnp.float32)  38.6 us
    all_gather x1, waiting for transfers between devices, body(): lax.all_gather(mirror_small[1], 'dp', axis=0, tiled=True)  31.7 us
    dot_general x12, matrix products, layer(): jnp.dot(scaled, w_up, preferred_element_type=jnp.float32)  28.2 us
  transfers between devices with their start and end apart: 28, of which 17 were waited for; matrix products, arithmetic and copies ran while one was open for 27% of the time, Pallas kernels for 0%

commit v1 on v0

v1 whole, which is shorter than its diff:
```python
import functools

import jax
import jax.numpy as jnp
from jax import lax
from jax.experimental import pallas as pl
from jax.experimental.pallas import tpu as pltpu
from jax.sharding import PartitionSpec as P

TICKS = 2
MESH = pl.DeviceIdType.MESH
BF16 = jnp.bfloat16
F32 = jnp.float32


def place():
    s, d = lax.axis_index("section"), lax.axis_index("dp")
    return s, d, lax.div(d, 2), lax.rem(d, 2)


def greet(sections, chips):
    s, d, z, c = place()
    barrier = pltpu.get_barrier_semaphore()

    def hello(section, index):
        pl.semaphore_signal(barrier, inc=1, device_id=(section, index), device_id_type=MESH)

    hello(sections - 1 - s, d)
    hello(s, d + 1 - 2 * c)

    @pl.when(z > 0)
    def _():
        hello(s, d - 2)

    @pl.when(z < chips - 1)
    def _():
        hello(s, d + 2)

    pl.semaphore_wait(barrier, 2 + jnp.minimum(z, 1) + jnp.minimum(chips - 1 - z, 1))


def down_at(full, e, rows):
    return full.at[pl.ds(pl.multiple_of(e * rows, 16), rows), :]


def up_at(full, e, columns):
    if len(full.shape) == 3:
        return full.at[e]
    return full.at[:, pl.ds(pl.multiple_of(e * columns, 128), columns)]


def remote(src, dst, send, recv, device):
    return pltpu.make_async_remote_copy(
        src_ref=src, dst_ref=dst, send_sem=send, recv_sem=recv, device_id=device, device_id_type=MESH
    )


def gather_kernel(
    sections, chips, wd, wu, gains, owd, owu, mwd, mwu, mgains, sems, local_sems, gain_sems
):
    s, d, z, c = place()
    width = wd.shape[0]
    mirror = (sections - 1 - s, d)
    sibling = (s, d + 1 - 2 * c)
    right, left = (s, d + 2), (s, d - 2)
    greet(sections, chips)

    def slot(full, p, chip, core):
        return (down_at, up_at)[p](full[p], chip * 2 + core, width)

    own, mir, shard = (owd, owu), (mwd, mwu), (wd, wu)

    def at(kind, p, chip):
        return sems.at[kind, p, chip]

    def line_copy(p, chip, src, kind, device):
        return remote(src, slot(own, p, chip, c), at(kind, p, chip), at(0, p, chip), device)

    def sibling_copy(p, chip, src):
        return remote(src, slot(own, p, chip, c), at(3, p, chip), at(4, p, chip), sibling)

    def mirror_copy(p, chip, src):
        return remote(src, slot(mir, p, chip, c), at(5, p, chip), at(6, p, chip), mirror)

    def mirror_sibling_copy(p, chip):
        block = slot(mir, p, chip, c)
        return remote(block, block, at(7, p, chip), at(8, p, chip), sibling)

    gain_copy = remote(gains, mgains, gain_sems.at[0], gain_sems.at[1], mirror)
    for p in range(2):
        pltpu.make_async_copy(shard[p], slot(own, p, z, c), local_sems.at[p]).start()

        @pl.when(z < chips - 1)
        def _():
            line_copy(p, z, shard[p], 1, right).start()

        @pl.when(z > 0)
        def _():
            line_copy(p, z, shard[p], 2, left).start()

        mirror_copy(p, z, shard[p]).start()
        sibling_copy(p, z, shard[p]).start()
    gain_copy.start()

    def pass_mirror(k):
        for p in range(2):
            for chip in (z - k, z + k)[: 1 if k == 0 else 2]:

                @pl.when((chip >= 0) & (chip < chips))
                def _():
                    mirror_copy(p, chip, slot(mir, p, chip, c)).wait_recv()
                    mirror_sibling_copy(p, chip).start()

    for k in range(1, chips):
        for p in range(2):

            @pl.when(z - k >= 0)
            def _():
                block = slot(own, p, z - k, c)
                line_copy(p, z - k, block, 1, right).wait_recv()

                @pl.when(z < chips - 1)
                def _():
                    line_copy(p, z - k, block, 1, right).start()

                mirror_copy(p, z - k, block).start()
                sibling_copy(p, z - k, block).start()

            @pl.when(z + k < chips)
            def _():
                block = slot(own, p, z + k, c)
                line_copy(p, z + k, block, 2, left).wait_recv()

                @pl.when(z > 0)
                def _():
                    line_copy(p, z + k, block, 2, left).start()

                mirror_copy(p, z + k, block).start()
                sibling_copy(p, z + k, block).start()

        pass_mirror(k - 1)
    pass_mirror(chips - 1)

    for p in range(2):
        pltpu.make_async_copy(shard[p], slot(own, p, z, c), local_sems.at[p]).wait()
        for chip in range(chips):
            theirs = slot(own, p, chip, 1 - c)
            remote(theirs, theirs, at(3, p, chip), at(4, p, chip), sibling).wait()
            mirror_copy(p, chip, slot(own, p, chip, c)).wait_send()
            theirs = slot(mir, p, chip, 1 - c)
            remote(theirs, theirs, at(7, p, chip), at(8, p, chip), sibling).wait()

            @pl.when((chip <= z) & (z < chips - 1))
            def _():
                line_copy(p, chip, slot(own, p, chip, c), 1, right).wait_send()

            @pl.when((chip >= z) & (z > 0))
            def _():
                line_copy(p, chip, slot(own, p, chip, c), 2, left).wait_send()

    gain_copy.wait()


def gather(sections, n_dp, wd, wu, gains):
    width, rank = wd.shape
    up_shape = (rank, n_dp * width) if width % 128 == 0 else (n_dp, rank, width)
    down = jax.ShapeDtypeStruct((n_dp * width, rank), wd.dtype)
    up = jax.ShapeDtypeStruct(up_shape, wu.dtype)
    chips = n_dp // 2
    owd, owu, mwd, mwu, mgains = pl.pallas_call(
        functools.partial(gather_kernel, sections, chips),
        out_shape=(down, up, down, up, jax.ShapeDtypeStruct(gains.shape, gains.dtype)),
        in_specs=[pl.BlockSpec(memory_space=pl.ANY)] * 3,
        out_specs=(pl.BlockSpec(memory_space=pl.ANY),) * 5,
        scratch_shapes=[
            pltpu.SemaphoreType.DMA((9, 2, chips)),
            pltpu.SemaphoreType.DMA((2,)),
            pltpu.SemaphoreType.DMA((2,)),
        ],
        compiler_params=pltpu.CompilerParams(
            collective_id=0, has_side_effects=True, vmem_limit_bytes=56 * 2**20
        ),
        name="gather_weights",
    )(wd, wu, gains)

    def whole(v):
        return v if v.ndim == 2 else v.transpose(1, 0, 2).reshape(rank, n_dp * width)

    return owd, whole(owu), mwd, whole(mwu), mgains


def reduce_kernel(sections, chips, ad, au, asm, bd, bu, bsm, od, ou, osm, *scratch):
    s, d, z, c = place()
    width = od.shape[0]
    mirror = (sections - 1 - s, d)
    sibling = (s, d + 1 - 2 * c)
    right, left = (s, d + 2), (s, d - 2)
    mine_a, mine_b, got_a, got_b, crossed, from_left, from_right = (
        scratch[3 * i : 3 * i + 3] for i in range(7)
    )
    sems = scratch[21]
    a, b, out = (ad, au, asm), (bd, bu, bsm), (od, ou, osm)

    def part(full, p, chip, core):
        e = chip * 2 + core
        if p == 0:
            return down_at(full[0], e, width)
        if p == 1:
            return up_at(full[1], e, width)
        return full[2].at[e]

    def at(kind, p, chip):
        return sems.at[kind, p, chip]

    def load(p, chip, full, mine, kind):
        return pltpu.make_async_copy(part(full, p, chip, c), mine[p].at[chip], at(kind, p, chip))

    def swap(p, chip, full, got, kind):
        return remote(
            part(full, p, chip, 1 - c), got[p].at[chip], at(kind, p, chip), at(kind + 1, p, chip), sibling
        )

    def cross(p, chip):
        return remote(mine_b[p].at[chip], crossed[p].at[chip], at(6, p, chip), at(7, p, chip), mirror)

    def to_right(p, chip):
        return remote(mine_a[p].at[chip], from_left[p].at[chip], at(8, p, chip), at(9, p, chip), right)

    def to_left(p, chip):
        return remote(mine_a[p].at[chip], from_right[p].at[chip], at(10, p, chip), at(11, p, chip), left)

    def add(p, chip, dst, terms):
        rows = terms[0][p].shape[1]
        step = rows if p == 2 else rows // 8 if rows % 128 == 0 else rows // 7

        def body(i, carry):
            at_rows = pl.ds(pl.multiple_of(i * step, 8 if p == 2 else 16), step)
            total = terms[0][p][chip, at_rows, :].astype(F32)
            for term in terms[1:]:
                total = total + term[p][chip, at_rows, :].astype(F32)
            if dst is out:
                dst[p][at_rows, :] = total
            else:
                dst[p][chip, at_rows, :] = total.astype(dst[p].dtype)
            return carry

        lax.fori_loop(0, rows // step, body, 0)

    def each(k, do):
        if k == 0:
            do(z, 0)
        else:

            @pl.when(z + k < chips)
            def _():
                do(z + k, 1)

            @pl.when(z - k >= 0)
            def _():
                do(z - k, -1)

    greet(sections, chips)
    far_first = list(range(chips - 1, -1, -1))
    for full, mine, got, kind, local in ((b, mine_b, got_b, 4, 1), (a, mine_a, got_a, 2, 0)):
        for k in far_first:

            def begin(chip, side):
                for p in range(3):
                    swap(p, chip, full, got, kind).start()
                    load(p, chip, full, mine, local).start()

            each(k, begin)
    for full, mine, got, kind, local in ((b, mine_b, got_b, 4, 1), (a, mine_a, got_a, 2, 0)):
        for k in far_first:

            def pair(chip, side):
                for p in range(3):
                    swap(p, chip, full, got, kind).wait_recv()
                    load(p, chip, full, mine, local).wait()
                    add(p, chip, mine, (mine, got))
                    if local == 1:
                        cross(p, chip).start()

            each(k, pair)

    for k in far_first:

        def onward(chip, side):
            for p in range(3):
                cross(p, chip).wait_recv()
                if side == 1:

                    @pl.when(z > 0)
                    def _():
                        to_right(p, chip).wait_recv()
                        add(p, chip, mine_a, (mine_a, crossed, from_left))

                    @pl.when(z == 0)
                    def _():
                        add(p, chip, mine_a, (mine_a, crossed))

                    to_right(p, chip).start()
                elif side == -1:

                    @pl.when(z < chips - 1)
                    def _():
                        to_left(p, chip).wait_recv()
                        add(p, chip, mine_a, (mine_a, crossed, from_right))

                    @pl.when(z == chips - 1)
                    def _():
                        add(p, chip, mine_a, (mine_a, crossed))

                    to_left(p, chip).start()
                else:

                    @pl.when(z > 0)
                    def _():
                        to_right(p, chip).wait_recv()

                    @pl.when(z < chips - 1)
                    def _():
                        to_left(p, chip).wait_recv()

                    @pl.when(z == 0)
                    def _():
                        add(p, chip, out, (mine_a, crossed, from_right))

                    @pl.when(z == chips - 1)
                    def _():
                        add(p, chip, out, (mine_a, crossed, from_left))

                    @pl.when((z > 0) & (z < chips - 1))
                    def _():
                        add(p, chip, out, (mine_a, crossed, from_left, from_right))

        each(k, onward)

    for k in far_first:

        def finish(chip, side):
            for p in range(3):
                swap(p, chip, a, got_a, 2).wait_send()
                swap(p, chip, b, got_b, 4).wait_send()
                cross(p, chip).wait_send()
                if side == 1:
                    to_right(p, chip).wait_send()
                elif side == -1:
                    to_left(p, chip).wait_send()

        each(k, finish)


def reduce_grads(sections, n_dp, grads_a, grads_b):
    total, rank = grads_a[0].shape
    width = total // n_dp
    chips = n_dp // 2

    def prepared(grads):
        norm, down, latent, up = grads[2], grads[0], grads[3], grads[1]
        if width % 128:
            up = up.reshape(rank, n_dp, width).transpose(1, 0, 2)
        small = jnp.concatenate([norm.reshape(n_dp, width), latent.reshape(n_dp, rank // n_dp)], axis=1)
        small = jnp.pad(small, ((0, 0), (0, 1024 - small.shape[1]))).reshape(n_dp, 8, 128)
        return down, up, small

    blocks = [
        pltpu.VMEM((chips, width, rank), BF16),
        pltpu.VMEM((chips, rank, width), BF16),
        pltpu.VMEM((chips, 8, 128), F32),
    ]
    down, up, small = pl.pallas_call(
        functools.partial(reduce_kernel, sections, chips),
        out_shape=(
            jax.ShapeDtypeStruct((width, rank), F32),
            jax.ShapeDtypeStruct((rank, width), F32),
            jax.ShapeDtypeStruct((8, 128), F32),
        ),
        in_specs=[pl.BlockSpec(memory_space=pl.ANY)] * 6,
        out_specs=(pl.BlockSpec(memory_space=pltpu.VMEM),) * 3,
        scratch_shapes=blocks * 7 + [pltpu.SemaphoreType.DMA((12, 3, chips))],
        compiler_params=pltpu.CompilerParams(
            collective_id=1, has_side_effects=True, vmem_limit_bytes=56 * 2**20
        ),
        name="reduce_grads",
    )(*prepared(grads_a), *prepared(grads_b))
    flat = small.reshape(1024)
    return flat[:width], down, flat[width : width + rank // n_dp], up


def from_behind(block, axis, distance):
    devices = range(lax.axis_size(axis))
    route = [(i - distance, i) for i in devices if i - distance in devices]
    return lax.ppermute(block, axis, route)


def dot(p, q, contract):
    return lax.dot_general(p, q, (contract, ((), ())), preferred_element_type=F32)


def inner(x, gain, wd, latent_gain):
    xf = x.astype(F32)
    r = lax.rsqrt(jnp.mean(xf * xf, axis=-1, keepdims=True) + 1e-06)
    normed = (xf * r * gain).astype(BF16)
    latent = dot(normed, wd, ((1,), (0,)))
    rl = lax.rsqrt(jnp.mean(latent * latent, axis=-1, keepdims=True) + 1e-06)
    scaled = (latent * rl * latent_gain).astype(BF16)
    return r, normed, latent, rl, scaled


def forward(x, weights):
    gain, wd, latent_gain, wu = weights
    scaled = inner(x, gain, wd, latent_gain)[4]
    return (x.astype(F32) + dot(scaled, wu, ((1,), (0,)))).astype(BF16)


def backward(x, g, saved, weights):
    gain, wd, latent_gain, wu = weights
    r, normed, latent, rl, scaled = saved
    d_scaled = dot(g, wu, ((1,), (1,)))
    d_latent_gain = jnp.sum(d_scaled * latent * rl, axis=0)
    d_hat = d_scaled * latent_gain
    d_latent = rl * (d_hat - latent * (rl * rl * jnp.mean(d_hat * latent, axis=-1, keepdims=True)))
    d_latent = d_latent.astype(BF16)
    d_down = dot(normed, d_latent, ((0,), (0,)))
    d_up = dot(scaled, g, ((0,), (0,)))
    d_normed = dot(d_latent, wd, ((1,), (1,))).astype(BF16).astype(F32)
    xf = x.astype(F32)
    d_gain = jnp.sum(d_normed * (xf * r), axis=0)
    d_unit = d_normed * gain
    back = g.astype(F32) + r * (
        d_unit - xf * (r * r * jnp.mean(d_unit * xf, axis=-1, keepdims=True))
    )
    return back.astype(BF16), (d_down, d_up, d_gain, d_latent_gain)


def body(
    enter_a, enter_b, cotan_a, cotan_b, saved_a, saved_b, norm_gain, w_down, latent_gain, w_up
):
    sections, n_dp = lax.axis_size("section"), lax.axis_size("dp")
    total, rank = norm_gain.shape[1], latent_gain.shape[1]
    gains = jnp.concatenate([norm_gain[0], latent_gain[0]])
    gains = jnp.pad(gains, (0, -gains.shape[0] % 1024)).reshape(-1, 128)
    owd, owu, mwd, mwu, mgains = gather(sections, n_dp, w_down[0], w_up[0], gains)
    mgains = mgains.reshape(-1)
    own = (norm_gain[0], owd, latent_gain[0], owu)
    mir = (mgains[:total], mwd, mgains[total : total + rank], mwu)

    def step(x, saved_x, g, weights):
        kept = inner(saved_x, weights[0], weights[1], weights[2])
        back, grads = backward(saved_x, g, kept, weights)
        return forward(x, weights), back, grads

    out_a, back_a, sum_a = step(enter_a[0], saved_a[0, 0], cotan_a[0], own)
    grad_a = from_behind(back_a, "section", -1)
    state_a = from_behind(out_a, "section", 1)
    out_b, back_b, sum_b = step(enter_b[0], saved_b[0, 0], cotan_b[0], mir)
    grad_b = from_behind(back_b, "section", 1)
    state_b = from_behind(out_b, "section", -1)

    out_a, back_a, more_a = step(state_a, saved_a[1, 0], grad_a, own)
    out_b, back_b, more_b = step(state_b, saved_b[1, 0], grad_b, mir)

    def summed(first, second):
        both = [p + q for p, q in zip(first, second)]
        rounded = [v.astype(BF16) for v in both]
        return rounded[0], rounded[1], rounded[2].astype(F32), rounded[3].astype(F32)

    norm, down, latent, up = reduce_grads(
        sections, n_dp, summed(sum_a, more_a), summed(sum_b, more_b)
    )
    return (
        out_a[None],
        out_b[None],
        back_a[None],
        back_b[None],
        norm[None],
        down[None],
        latent[None],
        up[None],
    )


def solution(mesh):
    placed = (
        P("section", "dp", None),
        P("section", "dp", None),
        P("section", "dp", None),
        P("section", "dp", None),
        P(None, "section", "dp", None),
        P(None, "section", "dp", None),
        P("section", None),
        P("section", "dp", None),
        P("section", None),
        P("section", None, "dp"),
    )
    return jax.shard_map(
        body,
        mesh=mesh,
        in_specs=placed,
        out_specs=(
            P("section", "dp", None),
            P("section", "dp", None),
            P("section", "dp", None),
            P("section", "dp", None),
            P("section", "dp"),
            P("section", "dp", None),
            P("section", "dp"),
            P("section", None, "dp"),
        ),
        check_vma=False,
    )
```

time: 510 us -> 412 us (0.81)
  the two profiles are of different devices: /device:TPU:0 before, /device:TPU:12 now
where the time goes in v1:
time: 412 us; the launch traced here: 407 us
  Pallas kernels  175 us (42%)
  matrix products  95.2 us (23%)
  waiting for transfers between devices  86.3 us (21%)
  other arithmetic  21.2 us (5%)
  starting transfers between devices  14.6 us (4%)
  local copies, waits for them, and re-layouts  13.5 us (3%)
    dot_general x28, matrix products, dot(): lax.dot_general(p, q, (contract, ((), ())), preferred_element_type=F32)  95.2 us
    pallas_call x1, Pallas kernels, reduce_grads(): pl.pallas_call(functools.partial(reduce_kernel, sections, chips), out_sha...  89.2 us
    ppermute x4, waiting for transfers between devices, from_behind(): return lax.ppermute(block, axis, route)  86.3 us
    pallas_call x1, Pallas kernels, gather(): pl.pallas_call(functools.partial(gather_kernel, sections, chips), out_sha...  85.6 us
    ppermute x4, starting transfers between devices, from_behind(): return lax.ppermute(block, axis, route)  14.6 us
    unnamed x104, local copies, waits for them, and re-layouts  9.38 us
  transfers between devices with their start and end apart: 4, of which 2 were waited for; matrix products, arithmetic and copies ran while one was open for 14% of the time, Pallas kernels for 0%

profile of v1, /device:TPU:12, one launch (start us, length us, event | category | flops | bytes accessed | tf_op | source)
XLA Modules:
  0.0 407.0 jit_solution(593387310221820285)
XLA Ops:
  2.0 85.6 %gather_weights.1 = (bf16[7168,256]{1,0:T(8,128)(2,1)}, bf16[256,7168]{1,0:T(8,128)(2,1)}, bf16[7168,256]{1,0:T(8,128)(2,1)}, bf16[256,7168]{1,0:T(8,128)(2,1)}, f32[64,128]{1,0:T(8,128)}) custom-call(bf16[896,256]{1,0:T(8,128)(2,1)} %bitcast.176, bf16[256,896]{1,0:T(8,128)(2,1)} %bitcast.177, f32[64,128]{1,0:T(8,128)} %fusion.134.gains), custom_call_target="tpu_custom_call" | custom-call | tf_op jit(solution)/shard_map/gather_weights/pallas_call | solution.py:170
  89.1 1.9 fusion.39
  91.0 3.5 multiply_reduce_fusion.13
  95.3 1.9 fusion.6
  97.2 3.5 collective-permute-start.1
  105.2 3.9 collective-permute-start
  115.6 2.3 collective-permute-start.3
  121.4 2.4 fusion.29
  123.9 2.3 fusion.47
  126.2 4.8 %collective-permute-start.2 = (bf16[128,7168]{1,0:T(8,128)(2,1)}, bf16[128,7168]{1,0:T(8,128)(2,1)S(1)}, u32[]{:S(2)}, u32[]{:S(2)}) collective-permute-start(bf16[128,7168]{1,0:T(8,128)(2,1)} %fusion.47), channel_id=1, source_target_pairs={{8,0},{16,8},{24,16},{9,1},{17,9},{25,17},{10,2},{18,10},{26,18},{... | collective-permute-start | bytes 5505032 | tf_op jit(solution)/shard_map/ppermute | solution.py:394
  131.0 2.9 multiply_reduce_fusion.5
  134.7 4.2 %fusion.100 = f32[7168,256]{1,0:T(8,128)} fusion(bf16[128,256]{1,0:T(8,128)(2,1)S(1)} %multiply_convert_fusion.7, f32[128]{0:T(128)S(1)} %add_rsqrt_fusion.7, f32[7168]{0:T(1024)S(1)} %bitcast.169, bf16[2,1,128,7168]{3,2,1,0:T(8,128)(2,1)S(1)} %copy-done.8), kind=kOutput, calls=%fused_computation.128 | convolution fusion | flops 473432064 | bytes 9269760 | tf_op jit(solution)/shard_map/dot_general | solution.py:398
  138.9 4.2 %fusion.107 = f32[7168,256]{1,0:T(8,128)} fusion(bf16[128,256]{1,0:T(8,128)(2,1)S(1)} %multiply_convert_fusion.5, f32[128]{0:T(128)S(1)} %add_rsqrt_fusion.3, f32[7168]{0:T(1024)S(1)} %slice_bitcast_fusion, bf16[2,1,128,7168]{3,2,1,0:T(8,128)(2,1)S(1)} %copy-done.5), kind=kOutput, calls=%fused_computation.131 | convolution fusion | flops 473432064 | bytes 9269760 | tf_op jit(solution)/shard_map/dot_general | solution.py:398
  143.1 4.2 %fusion.76 = f32[256,7168]{1,0:T(8,128)} fusion(bf16[1,128,7168]{2,1,0:T(8,128)(2,1)S(1)} %copy-done.15, f32[128,256]{1,0:T(8,128)S(1)} %get-tuple-element.59, f32[128]{0:T(128)S(1)} %add_rsqrt_fusion.2, f32[256]{0:T(256)S(1)} %slice_bitcast_fusion.2), kind=kOutput, calls=%fused_computation.108 | convolution fusion | flops 469860352 | bytes 9307648 | tf_op jit(solution)/shard_map/dot_general | solution.py:398
  147.4 4.2 %fusion.80 = f32[256,7168]{1,0:T(8,128)} fusion(bf16[1,128,7168]{2,1,0:T(8,128)(2,1)S(1)} %copy-done.16, f32[128,256]{1,0:T(8,128)S(1)} %get-tuple-element.51, f32[128]{0:T(128)S(1)} %add_rsqrt_fusion.6, f32[256]{0:T(256)S(1)} %bitcast.184), kind=kOutput, calls=%fused_computation.112 | convolution fusion | flops 469860352 | bytes 9307648 | tf_op jit(solution)/shard_map/dot_general | solution.py:398
  151.6 70.3 %collective-permute-done.3 = bf16[128,7168]{1,0:T(8,128)(2,1)S(1)} collective-permute-done((bf16[128,7168]{1,0:T(8,128)(2,1)S(1)}, bf16[128,7168]{1,0:T(8,128)(2,1)S(1)}, u32[]{:S(2)}, u32[]{:S(2)}) %collective-permute-start.3) | collective-permute-done | bytes 1835040 | tf_op jit(solution)/shard_map/ppermute | solution.py:394
  223.5 5.9 %fusion.23 = (f32[7168]{0:T(1024)S(1)}, f32[128]{0:T(128)S(1)}, f32[128,7168]{1,0:T(8,128)}) fusion(f32[128]{0:T(128)S(1)} %add_rsqrt_fusion.1, bf16[2,1,128,7168]{3,2,1,0:T(8,128)(2,1)} %param.15, f32[7168]{0:T(1024)S(1)} %slice_bitcast_fusion, bf16[128,256]{1,0:T(8,128)(2,1)S(1)} %multiply_convert_fusion.4, bf16[7168,256]{1,0:T(8,128)(2,1)} %get-tuple-element.19), kind=kOutput, calls=%fused_computation.59 | convolution fusion | flops 478012288 | bytes 9298944 | tf_op jit(solution)/shard_map/dot_general | solution.py:398
  230.2 1.9 fusion.33
  232.1 4.1 %multiply_reduce_fusion.12 = (f32[128]{0:T(128)S(1)}, f32[128,256]{1,0:T(8,128)}) fusion(bf16[7168,256]{1,0:T(8,128)(2,1)} %get-tuple-element.19, bf16[128,7168]{1,0:T(8,128)(2,1)} %collective-permute-done.1, f32[128]{0:T(128)S(1)} %add_rsqrt_fusion.9, f32[7168]{0:T(1024)S(1)} %slice_bitcast_fusion), kind=kOutput, calls=%fused_computation.155 | convolution fusion | flops 473497472 | bytes 5665792 | tf_op jit(solution)/shard_map/dot_general | solution.py:398
  236.8 1.9 fusion.30
  238.7 3.0 multiply_reduce_fusion.14
  242.8 15.9 %collective-permute-done.2 = bf16[128,7168]{1,0:T(8,128)(2,1)S(1)} collective-permute-done((bf16[128,7168]{1,0:T(8,128)(2,1)}, bf16[128,7168]{1,0:T(8,128)(2,1)S(1)}, u32[]{:S(2)}, u32[]{:S(2)}) %collective-permute-start.2) | collective-permute-done | bytes 1835040 | tf_op jit(solution)/shard_map/ppermute | solution.py:394
  261.1 15.1 %fusion.27 = (f32[7168]{0:T(1024)S(1)}, f32[128]{0:T(128)}, f32[128,7168]{1,0:T(8,128)}) fusion(f32[128]{0:T(128)S(1)} %add_rsqrt_fusion.5, bf16[2,1,128,7168]{3,2,1,0:T(8,128)(2,1)} %param.14, f32[7168]{0:T(1024)S(1)} %bitcast.171, bf16[128,256]{1,0:T(8,128)(2,1)S(1)} %multiply_convert_fusion.6, bf16[7168,256]{1,0:T(8,128)(2,1)} %get-tuple-element.16), kind=kOutput, calls=%fused_computation.63 | convolution fusion | flops 478012288 | bytes 9298944 | tf_op jit(solution)/shard_map/dot_general | solution.py:398
  280.0 7.0 %fusion.ad = bf16[7168,256]{1,0:T(8,128)(2,1)} fusion(f32[7168,256]{1,0:T(8,128)} %fusion.100, bf16[128,256]{1,0:T(8,128)(2,1)} %copy-done.24, f32[128]{0:T(128)} %copy-done.33, f32[7168]{0:T(1024)S(1)} %bitcast.172, bf16[2,1,128,7168]{3,2,1,0:T(8,128)(2,1)} %param.14), kind=kOutput, calls=%fused_computation.4 | convolution fusion | flops 477102080 | bytes 12939776 | tf_op jit(solution)/shard_map/dot_general | solution.py:398
  287.1 3.1 fusion.2.bd
  290.3 6.4 %fusion.3.bu = bf16[256,7168]{1,0:T(8,128)(2,1)} fusion(f32[256,7168]{1,0:T(8,128)} %fusion.76, bf16[128,7168]{1,0:T(8,128)(2,1)S(1)} %copy-done.11, f32[128,256]{1,0:T(8,128)S(1)} %get-tuple-element.63, f32[128]{0:T(128)S(1)} %copy-done.30, f32[256]{0:T(256)S(1)} %slice_bitcast_fusion.2), kind=kOutput, calls=%fused_computation.7 | convolution fusion | flops 473530368 | bytes 12977664 | tf_op jit(solution)/shard_map/dot_general | solution.py:398
  296.6 3.1 fusion.1.au
  299.8 89.2 %reduce_grads.1 = (f32[896,256]{1,0:T(8,128)}, f32[256,896]{1,0:T(8,128)}, f32[8,128]{1,0:T(8,128)}) custom-call(bf16[7168,256]{1,0:T(8,128)(2,1)} %fusion.ad, bf16[256,7168]{1,0:T(8,128)(2,1)} %fusion.1.au, f32[8,8,128]{2,1,0:T(8,128)} %bitcast.179, bf16[7168,256]{1,0:T(8,128)(2,1)} %fusion.2.bd, bf16[256,7168]{1,0:T(8,128)(2,1)} %fusion.3.bu, ...), custom_call_target="tpu_custom_call" | custom-call | tf_op jit(solution)/shard_map/reduce_grads/pallas_call | solution.py:372
  391.5 3.6 fusion.12
  395.1 3.6 fusion.13
  398.8 2.3 fusion.66
  402.6 2.3 fusion.67
  (164 shorter events, 34.6 us)
Async XLA Ops:
  91.0 4.2 %copy-start.17 = (bf16[1,128,7168]{2,1,0:T(8,128)(2,1)S(1)}, bf16[1,128,7168]{2,1,0:T(8,128)(2,1)}, u32[]{:S(2)}) copy-start(bf16[1,128,7168]{2,1,0:T(8,128)(2,1)} %param.11) | copy-start | bytes 5505028
  95.3 5.5 %copy-start.18 = (bf16[1,128,7168]{2,1,0:T(8,128)(2,1)S(1)}, bf16[1,128,7168]{2,1,0:T(8,128)(2,1)}, u32[]{:S(2)}) copy-start(bf16[1,128,7168]{2,1,0:T(8,128)(2,1)} %param.10) | copy-start | bytes 5505028
  95.3 6.0 %copy-start.21 = (f32[1,7168]{1,0:T(1,128)S(1)}, f32[1,7168]{1,0:T(1,128)}, u32[]{:S(2)}) copy-start(f32[1,7168]{1,0:T(1,128)} %param.16) | copy-start | bytes 86020
  95.3 6.0 %copy-start.41 = (bf16[7168,256]{1,0:T(8,128)(2,1)S(1)}, bf16[7168,256]{1,0:T(8,128)(2,1)}, u32[]{:S(2)}) copy-start(bf16[7168,256]{1,0:T(8,128)(2,1)} %get-tuple-element.16) | copy-start | bytes 11010052
  97.2 133.0 %collective-permute-start.1 = (bf16[128,7168]{1,0:T(8,128)(2,1)}, bf16[128,7168]{1,0:T(8,128)(2,1)}, u32[]{:S(2)}, u32[]{:S(2)}) collective-permute-start(bf16[128,7168]{1,0:T(8,128)(2,1)} %fusion.6), channel_id=1, source_target_pairs={{8,0},{16,8},{24,16},{9,1},{17,9},{25,17},{10,2},{18,10},{26,18},{... | collective-permute-start | bytes 5505032 | tf_op jit(solution)/shard_map/ppermute | solution.py:394
  103.2 5.9 %copy-start.5 = (bf16[2,1,128,7168]{3,2,1,0:T(8,128)(2,1)S(1)}, bf16[2,1,128,7168]{3,2,1,0:T(8,128)(2,1)}, u32[]{:S(2)}) copy-start(bf16[2,1,128,7168]{3,2,1,0:T(8,128)(2,1)} %param.15) | copy-start | bytes 11010052
  103.2 6.3 %copy-start.43 = (bf16[7168,256]{1,0:T(8,128)(2,1)S(1)}, bf16[7168,256]{1,0:T(8,128)(2,1)}, u32[]{:S(2)}) copy-start(bf16[7168,256]{1,0:T(8,128)(2,1)} %get-tuple-element.19) | copy-start | bytes 11010052
  105.2 131.6 %collective-permute-start = (bf16[128,7168]{1,0:T(8,128)(2,1)}, bf16[128,7168]{1,0:T(8,128)(2,1)}, u32[]{:S(2)}, u32[]{:S(2)}) collective-permute-start(bf16[128,7168]{1,0:T(8,128)(2,1)} %fusion.4), channel_id=1, source_target_pairs={{0,8},{8,16},{16,24},{1,9},{9,17},{17,25},{2,10},{10,18},{18,26},{... | collective-permute-start | bytes 5505032 | tf_op jit(solution)/shard_map/ppermute | solution.py:394
  115.6 106.3 %collective-permute-start.3 = (bf16[128,7168]{1,0:T(8,128)(2,1)S(1)}, bf16[128,7168]{1,0:T(8,128)(2,1)S(1)}, u32[]{:S(2)}, u32[]{:S(2)}) collective-permute-start(bf16[128,7168]{1,0:T(8,128)(2,1)S(1)} %fusion.59), channel_id=1, source_target_pairs={{0,8},{8,16},{16,24},{1,9},{9,17},{17,25},{2,10},{10,18},{18,26},{... | collective-permute-start | bytes 5505032 | tf_op jit(solution)/shard_map/ppermute | solution.py:394
  123.8 10.1 %copy-start.44 = (f32[128]{0:T(128)}, f32[128]{0:T(128)S(1)}, u32[]{:S(2)}) copy-start(f32[128]{0:T(128)S(1)} %get-tuple-element.33) | copy-start | bytes 1540
  126.2 132.6 %collective-permute-start.2 = (bf16[128,7168]{1,0:T(8,128)(2,1)}, bf16[128,7168]{1,0:T(8,128)(2,1)S(1)}, u32[]{:S(2)}, u32[]{:S(2)}) collective-permute-start(bf16[128,7168]{1,0:T(8,128)(2,1)} %fusion.47), channel_id=1, source_target_pairs={{8,0},{16,8},{24,16},{9,1},{17,9},{25,17},{10,2},{18,10},{26,18},{... | collective-permute-start | bytes 5505032 | tf_op jit(solution)/shard_map/ppermute | solution.py:394
  131.0 92.5 %copy-start.35 = (f32[128]{0:T(128)}, f32[128]{0:T(128)S(1)}, u32[]{:S(2)}) copy-start(f32[128]{0:T(128)S(1)} %add_rsqrt_fusion.1) | copy-start | bytes 1540
  133.9 89.5 %copy-start.29 = (f32[128]{0:T(128)}, f32[128]{0:T(128)S(1)}, u32[]{:S(2)}) copy-start(f32[128]{0:T(128)S(1)} %add_rsqrt_fusion) | copy-start | bytes 1540
  133.9 127.1 %copy-start.33 = (f32[128]{0:T(128)}, f32[128]{0:T(128)S(1)}, u32[]{:S(2)}) copy-start(f32[128]{0:T(128)S(1)} %add_rsqrt_fusion.5) | copy-start | bytes 1540
  134.7 126.2 %copy-start.31 = (f32[128]{0:T(128)}, f32[128]{0:T(128)S(1)}, u32[]{:S(2)}) copy-start(f32[128]{0:T(128)S(1)} %add_rsqrt_fusion.4) | copy-start | bytes 1540
  232.1 6.6 %copy-start.42 = (bf16[7168,256]{1,0:T(8,128)(2,1)S(1)}, bf16[7168,256]{1,0:T(8,128)(2,1)}, u32[]{:S(2)}) copy-start(bf16[7168,256]{1,0:T(8,128)(2,1)} %get-tuple-element.16) | copy-start | bytes 11010052
  238.7 20.1 %copy-start.1 = (bf16[256,7168]{1,0:T(8,128)(2,1)S(1)}, bf16[256,7168]{1,0:T(8,128)(2,1)}, u32[]{:S(2)}) copy-start(bf16[256,7168]{1,0:T(8,128)(2,1)} %get-tuple-element.17) | copy-start | bytes 11010052
  261.0 15.1 %copy-start.24 = (bf16[128,256]{1,0:T(8,128)(2,1)}, bf16[128,256]{1,0:T(8,128)(2,1)S(1)}, u32[]{:S(2)}) copy-start(bf16[128,256]{1,0:T(8,128)(2,1)S(1)} %multiply_convert_fusion.6) | copy-start | bytes 196612
  261.1 15.1 %copy-start.28 = (f32[7168]{0:T(1024)S(1)}, f32[7168]{0:T(1024)}, u32[]{:S(2)}) copy-start(f32[7168]{0:T(1024)} %get-tuple-element.30) | copy-start | bytes 86020
  261.1 26.0 %slice-start = ((s8[7340032]{0:T(1024)(128)(4,1)}), s8[3145728]{0:T(1024)(128)(4,1)S(1)}, s32[]{:S(2)}) async-start(s8[7340032]{0:T(1024)(128)(4,1)} %bitcast.159), calls=%async_computation | async-start | bytes 6291456
  280.0 7.0 %slice-start.1 = ((s8[7340032]{0:T(1024)(128)(4,1)}), s8[4194304]{0:T(1024)(128)(4,1)S(1)}, s32[]{:S(2)}) async-start(s8[7340032]{0:T(1024)(128)(4,1)} %bitcast.159), calls=%async_computation.1 | async-start | bytes 8388608
  280.0 7.0 %copy-start.6 = (bf16[2,1,128,7168]{3,2,1,0:T(8,128)(2,1)S(1)}, bf16[2,1,128,7168]{3,2,1,0:T(8,128)(2,1)}, u32[]{:S(2)}) copy-start(bf16[2,1,128,7168]{3,2,1,0:T(8,128)(2,1)} %param.15) | copy-start | bytes 11010052
  280.0 7.0 %copy-start.36 = (f32[128]{0:T(128)S(1)}, f32[128]{0:T(128)}, u32[]{:S(2)}) copy-start(f32[128]{0:T(128)} %copy-done.35) | copy-start | bytes 1540
  287.1 9.5 %slice-start.2 = ((s8[7340032]{0:T(1024)(128)(4,1)}), s8[3145728]{0:T(1024)(128)(4,1)S(1)}, s32[]{:S(2)}) async-start(s8[7340032]{0:T(1024)(128)(4,1)} %bitcast.161), calls=%async_computation.2 | async-start | bytes 6291456
  290.2 6.4 %slice-start.3 = ((s8[7340032]{0:T(1024)(128)(4,1)}), s8[4194304]{0:T(1024)(128)(4,1)S(1)}, s32[]{:S(2)}) async-start(s8[7340032]{0:T(1024)(128)(4,1)} %bitcast.161), calls=%async_computation.3 | async-start | bytes 8388608
  290.2 6.4 %copy-start.14 = (bf16[128,7168]{1,0:T(8,128)(2,1)S(1)}, bf16[128,7168]{1,0:T(8,128)(2,1)}, u32[]{:S(2)}) copy-start(bf16[128,7168]{1,0:T(8,128)(2,1)} %copy-done.13) | copy-start | bytes 5505028
  290.2 6.4 %copy-start.32 = (f32[128]{0:T(128)S(1)}, f32[128]{0:T(128)}, u32[]{:S(2)}) copy-start(f32[128]{0:T(128)} %copy-done.31) | copy-start | bytes 1540
  299.8 91.7 %copy-start.4 = (bf16[256,7168]{1,0:T(8,128)(2,1)S(1)}, bf16[256,7168]{1,0:T(8,128)(2,1)}, u32[]{:S(2)}) copy-start(bf16[256,7168]{1,0:T(8,128)(2,1)} %get-tuple-element.20) | copy-start | bytes 11010052
  299.8 91.7 %copy-start.25 = (f32[128,256]{1,0:T(8,128)S(1)}, f32[128,256]{1,0:T(8,128)}, u32[]{:S(2)}) copy-start(f32[128,256]{1,0:T(8,128)} %get-tuple-element.49) | copy-start | bytes 393220
  299.8 91.7 %copy-start.37 = (f32[128]{0:T(128)S(1)}, f32[128]{0:T(128)}, u32[]{:S(2)}) copy-start(f32[128]{0:T(128)} %add_rsqrt_fusion.8) | copy-start | bytes 1540
  391.5 7.3 %copy-start.19 = (f32[128,7168]{1,0:T(8,128)S(1)}, f32[128,7168]{1,0:T(8,128)}, u32[]{:S(2)}) copy-start(f32[128,7168]{1,0:T(8,128)} %get-tuple-element.65) | copy-start | bytes 11010052
  398.8 3.8 copy-start.20
  (21 other events, 61.4 us)

commit v2 on v1

--- a/solution.py
+++ b/solution.py
@@ -86,6 +86,11 @@
         block = slot(mir, p, chip, c)
         return remote(block, block, at(7, p, chip), at(8, p, chip), sibling)
 
+    def mirror_line_copy(chip, toward):
+        kind, device = (9, right) if toward == 1 else (11, left)
+        block = slot(mir, 1, chip, c)
+        return remote(block, block, at(kind, 1, chip), at(kind + 1, 1, chip), device)
+
     gain_copy = remote(gains, mgains, gain_sems.at[0], gain_sems.at[1], mirror)
     for p in range(2):
         pltpu.make_async_copy(shard[p], slot(own, p, z, c), local_sems.at[p]).start()
@@ -104,12 +109,25 @@
 
     def pass_mirror(k):
         for p in range(2):
-            for chip in (z - k, z + k)[: 1 if k == 0 else 2]:
+            for side, chip in enumerate((z - k, z + k)[: 1 if k == 0 else 2]):
 
                 @pl.when((chip >= 0) & (chip < chips))
                 def _():
-                    mirror_copy(p, chip, slot(mir, p, chip, c)).wait_recv()
+                    if k == 1 and p == 1:
+                        mirror_line_copy(chip, 1 if side == 0 else -1).wait_recv()
+                    else:
+                        mirror_copy(p, chip, slot(mir, p, chip, c)).wait_recv()
                     mirror_sibling_copy(p, chip).start()
+
+                if k == 0 and p == 1:
+
+                    @pl.when(z < chips - 1)
+                    def _():
+                        mirror_line_copy(z, 1).start()
+
+                    @pl.when(z > 0)
+                    def _():
+                        mirror_line_copy(z, -1).start()
 
     for k in range(1, chips):
         for p in range(2):
@@ -123,7 +141,8 @@
                 def _():
                     line_copy(p, z - k, block, 1, right).start()
 
-                mirror_copy(p, z - k, block).start()
+                if k > 1 or p == 0:
+                    mirror_copy(p, z - k, block).start()
                 sibling_copy(p, z - k, block).start()
 
             @pl.when(z + k < chips)
@@ -135,7 +154,8 @@
                 def _():
                     line_copy(p, z + k, block, 2, left).start()
 
-                mirror_copy(p, z + k, block).start()
+                if k > 1 or p == 0:
+                    mirror_copy(p, z + k, block).start()
                 sibling_copy(p, z + k, block).start()
 
         pass_mirror(k - 1)
@@ -146,7 +166,14 @@
         for chip in range(chips):
             theirs = slot(own, p, chip, 1 - c)
             remote(theirs, theirs, at(3, p, chip), at(4, p, chip), sibling).wait()
-            mirror_copy(p, chip, slot(own, p, chip, c)).wait_send()
+            if p == 0:
+                mirror_copy(p, chip, slot(own, p, chip, c)).wait_send()
+            else:
+
+                @pl.when((chip != z + 1) & (chip != z - 1))
+                def _():
+                    mirror_copy(p, chip, slot(own, p, chip, c)).wait_send()
+
             theirs = slot(mir, p, chip, 1 - c)
             remote(theirs, theirs, at(7, p, chip), at(8, p, chip), sibling).wait()
 
@@ -157,6 +184,14 @@
             @pl.when((chip >= z) & (z > 0))
             def _():
                 line_copy(p, chip, slot(own, p, chip, c), 2, left).wait_send()
+
+    @pl.when(z < chips - 1)
+    def _():
+        mirror_line_copy(z, 1).wait_send()
+
+    @pl.when(z > 0)
+    def _():
+        mirror_line_copy(z, -1).wait_send()
 
     gain_copy.wait()
 
@@ -173,7 +208,7 @@
         in_specs=[pl.BlockSpec(memory_space=pl.ANY)] * 3,
         out_specs=(pl.BlockSpec(memory_space=pl.ANY),) * 5,
         scratch_shapes=[
-            pltpu.SemaphoreType.DMA((9, 2, chips)),
+            pltpu.SemaphoreType.DMA((13, 2, chips)),
             pltpu.SemaphoreType.DMA((2,)),
             pltpu.SemaphoreType.DMA((2,)),
         ],
@@ -198,7 +233,7 @@
     mine_a, mine_b, got_a, got_b, crossed, from_left, from_right = (
         scratch[3 * i : 3 * i + 3] for i in range(7)
     )
-    sems = scratch[21]
+    sems, left_b, right_b = scratch[21:24]
     a, b, out = (ad, au, asm), (bd, bu, bsm), (od, ou, osm)
 
     def part(full, p, chip, core):
@@ -223,11 +258,17 @@
     def cross(p, chip):
         return remote(mine_b[p].at[chip], crossed[p].at[chip], at(6, p, chip), at(7, p, chip), mirror)
 
-    def to_right(p, chip):
-        return remote(mine_a[p].at[chip], from_left[p].at[chip], at(8, p, chip), at(9, p, chip), right)
-
-    def to_left(p, chip):
-        return remote(mine_a[p].at[chip], from_right[p].at[chip], at(10, p, chip), at(11, p, chip), left)
+    def to_right(p, chip, stream=0):
+        kind, mine, lands = ((8, mine_a, from_left), (12, mine_b, {1: left_b}))[stream]
+        return remote(
+            mine[p].at[chip], lands[p].at[chip], at(kind, p, chip), at(kind + 1, p, chip), right
+        )
+
+    def to_left(p, chip, stream=0):
+        kind, mine, lands = ((10, mine_a, from_right), (14, mine_b, {1: right_b}))[stream]
+        return remote(
+            mine[p].at[chip], lands[p].at[chip], at(kind, p, chip), at(kind + 1, p, chip), left
+        )
 
     def add(p, chip, dst, terms):
         rows = terms[0][p].shape[1]
@@ -278,61 +319,85 @@
                     swap(p, chip, full, got, kind).wait_recv()
                     load(p, chip, full, mine, local).wait()
                     add(p, chip, mine, (mine, got))
-                    if local == 1:
+                    if local == 1 and p != 1:
                         cross(p, chip).start()
 
             each(k, pair)
 
+    def pass_on(p, chip, side, stream, terms):
+        mine = (mine_a, mine_b)[stream]
+        lands_left = (from_left, {1: left_b})[stream]
+        lands_right = (from_right, {1: right_b})[stream]
+        first, last = z == 0, z == chips - 1
+        if side == 1:
+
+            @pl.when(jnp.logical_not(first))
+            def _():
+                to_right(p, chip, stream).wait_recv()
+                add(p, chip, mine, terms + (lands_left,))
+
+            if len(terms) > 1:
+
+                @pl.when(first)
+                def _():
+                    add(p, chip, mine, terms)
+
+            to_right(p, chip, stream).start()
+        elif side == -1:
+
+            @pl.when(jnp.logical_not(last))
+            def _():
+                to_left(p, chip, stream).wait_recv()
+                add(p, chip, mine, terms + (lands_right,))
+
+            if len(terms) > 1:
+
+                @pl.when(last)
+                def _():
+                    add(p, chip, mine, terms)
+
+            to_left(p, chip, stream).start()
+        else:
+
+            @pl.when(jnp.logical_not(first))
+            def _():
+                to_right(p, chip, stream).wait_recv()
+
+            @pl.when(jnp.logical_not(last))
+            def _():
+                to_left(p, chip, stream).wait_recv()
+
+            if stream == 0 and p == 1:
+                cross(p, chip).wait_recv()
+                terms = terms + (crossed,)
+            dst = (out, mine_b)[stream]
+
+            @pl.when(first)
+            def _():
+                add(p, chip, dst, terms + (lands_right,))
+
+            @pl.when(last)
+            def _():
+                add(p, chip, dst, terms + (lands_left,))
+
+            @pl.when(jnp.logical_not(first) & jnp.logical_not(last))
+            def _():
+                add(p, chip, dst, terms + (lands_left, lands_right))
+
+            if stream == 1:
+                cross(p, chip).start()
+
     for k in far_first:
 
         def onward(chip, side):
-            for p in range(3):
+            pass_on(1, chip, side, 1, (mine_b,))
+            if side:
+                pass_on(1, chip, side, 0, (mine_a,))
+            for p in (0, 2):
                 cross(p, chip).wait_recv()
-                if side == 1:
-
-                    @pl.when(z > 0)
-                    def _():
-                        to_right(p, chip).wait_recv()
-                        add(p, chip, mine_a, (mine_a, crossed, from_left))
-
-                    @pl.when(z == 0)
-                    def _():
-                        add(p, chip, mine_a, (mine_a, crossed))
-
-                    to_right(p, chip).start()
-                elif side == -1:
-
-                    @pl.when(z < chips - 1)
-                    def _():
-                        to_left(p, chip).wait_recv()
-                        add(p, chip, mine_a, (mine_a, crossed, from_right))
-
-                    @pl.when(z == chips - 1)
-                    def _():
-                        add(p, chip, mine_a, (mine_a, crossed))
-
-                    to_left(p, chip).start()
-                else:
-
-                    @pl.when(z > 0)
-                    def _():
-                        to_right(p, chip).wait_recv()
-
-                    @pl.when(z < chips - 1)
-                    def _():
-                        to_left(p, chip).wait_recv()
-
-                    @pl.when(z == 0)
-                    def _():
-                        add(p, chip, out, (mine_a, crossed, from_right))
-
-                    @pl.when(z == chips - 1)
-                    def _():
-                        add(p, chip, out, (mine_a, crossed, from_left))
-
-                    @pl.when((z > 0) & (z < chips - 1))
-                    def _():
-                        add(p, chip, out, (mine_a, crossed, from_left, from_right))
+                pass_on(p, chip, side, 0, (mine_a, crossed))
+            if not side:
+                pass_on(1, chip, side, 0, (mine_a,))
 
         each(k, onward)
 
@@ -342,11 +407,13 @@
             for p in range(3):
                 swap(p, chip, a, got_a, 2).wait_send()
                 swap(p, chip, b, got_b, 4).wait_send()
-                cross(p, chip).wait_send()
-                if side == 1:
-                    to_right(p, chip).wait_send()
-                elif side == -1:
-                    to_left(p, chip).wait_send()
+                if p != 1 or side == 0:
+                    cross(p, chip).wait_send()
+                for stream in range(2 if p == 1 else 1):
+                    if side == 1:
+                        to_right(p, chip, stream).wait_send()
+                    elif side == -1:
+                        to_left(p, chip, stream).wait_send()
 
         each(k, finish)
 
@@ -378,10 +445,11 @@
         ),
         in_specs=[pl.BlockSpec(memory_space=pl.ANY)] * 6,
         out_specs=(pl.BlockSpec(memory_space=pltpu.VMEM),) * 3,
-        scratch_shapes=blocks * 7 + [pltpu.SemaphoreType.DMA((12, 3, chips))],
+        scratch_shapes=blocks * 7 + [pltpu.SemaphoreType.DMA((16, 3, chips))] + blocks[1:2] * 2,
         compiler_params=pltpu.CompilerParams(
             collective_id=1, has_side_effects=True, vmem_limit_bytes=56 * 2**20
         ),
+        cost_estimate=pl.CostEstimate(flops=0, bytes_accessed=10**6, transcendentals=0),
         name="reduce_grads",
     )(*prepared(grads_a), *prepared(grads_b))
     flat = small.reshape(1024)
@@ -414,24 +482,23 @@
     return (x.astype(F32) + dot(scaled, wu, ((1,), (0,)))).astype(BF16)
 
 
-def backward(x, g, saved, weights):
+def latent_grads(g, latent, rl, weights):
     gain, wd, latent_gain, wu = weights
-    r, normed, latent, rl, scaled = saved
     d_scaled = dot(g, wu, ((1,), (1,)))
     d_latent_gain = jnp.sum(d_scaled * latent * rl, axis=0)
     d_hat = d_scaled * latent_gain
     d_latent = rl * (d_hat - latent * (rl * rl * jnp.mean(d_hat * latent, axis=-1, keepdims=True)))
-    d_latent = d_latent.astype(BF16)
-    d_down = dot(normed, d_latent, ((0,), (0,)))
-    d_up = dot(scaled, g, ((0,), (0,)))
+    along = jnp.sum(d_latent * latent, axis=-1, keepdims=True)
+    return d_latent.astype(BF16), along, d_latent_gain
+
+
+def input_grads(x, g, r, d_latent, along, weights):
+    gain, wd = weights[:2]
     d_normed = dot(d_latent, wd, ((1,), (1,))).astype(BF16).astype(F32)
-    xf = x.astype(F32)
-    d_gain = jnp.sum(d_normed * (xf * r), axis=0)
-    d_unit = d_normed * gain
-    back = g.astype(F32) + r * (
-        d_unit - xf * (r * r * jnp.mean(d_unit * xf, axis=-1, keepdims=True))
-    )
-    return back.astype(BF16), (d_down, d_up, d_gain, d_latent_gain)
+    unit = x.astype(F32) * r
+    d_gain = jnp.sum(d_normed * unit, axis=0)
+    back = g.astype(F32) + r * (d_normed * gain - unit * (along / x.shape[1]))
+    return back.astype(BF16), d_gain
 
 
 def body(
@@ -446,29 +513,42 @@
     own = (norm_gain[0], owd, latent_gain[0], owu)
     mir = (mgains[:total], mwd, mgains[total : total + rank], mwu)
 
-    def step(x, saved_x, g, weights):
-        kept = inner(saved_x, weights[0], weights[1], weights[2])
-        back, grads = backward(saved_x, g, kept, weights)
-        return forward(x, weights), back, grads
-
-    out_a, back_a, sum_a = step(enter_a[0], saved_a[0, 0], cotan_a[0], own)
+    def first_back(saved, g, weights):
+        kept = inner(saved[0, 0], *weights[:3])
+        r, normed, latent, rl, scaled = kept
+        d_latent, along, d_latent_gain = latent_grads(g, latent, rl, weights)
+        back, d_gain = input_grads(saved[0, 0], g, r, d_latent, along, weights)
+        return back, (normed, d_latent, scaled, g, d_gain, d_latent_gain)
+
+    def second_back(saved, g, weights, first, kept):
+        r, normed, latent, rl, scaled = kept
+        d_latent, along, d_latent_gain = latent_grads(g, latent, rl, weights)
+        back, d_gain = input_grads(saved[1, 0], g, r, d_latent, along, weights)
+        down = dot(first[0], first[1], ((0,), (0,))) + dot(normed, d_latent, ((0,), (0,)))
+        up = dot(first[2], first[3], ((0,), (0,))) + dot(scaled, g, ((0,), (0,)))
+        small = [(p + q).astype(BF16).astype(F32) for p, q in zip(first[4:], (d_gain, d_latent_gain))]
+        return back, (down.astype(BF16), up.astype(BF16), *small)
+
+    back_a, first_a = first_back(saved_a, cotan_a[0], own)
     grad_a = from_behind(back_a, "section", -1)
+    back_b, first_b = first_back(saved_b, cotan_b[0], mir)
+    grad_b = from_behind(back_b, "section", 1)
+    out_a = forward(enter_a[0], own)
+    out_b = forward(enter_b[0], mir)
+    kept_a = inner(saved_a[1, 0], *own[:3])
+    kept_b = inner(saved_b[1, 0], *mir[:3])
+    grad_a, grad_b, out_a, out_b, kept_a, kept_b = lax.optimization_barrier(
+        (grad_a, grad_b, out_a, out_b, kept_a, kept_b)
+    )
     state_a = from_behind(out_a, "section", 1)
-    out_b, back_b, sum_b = step(enter_b[0], saved_b[0, 0], cotan_b[0], mir)
-    grad_b = from_behind(back_b, "section", 1)
     state_b = from_behind(out_b, "section", -1)
-
-    out_a, back_a, more_a = step(state_a, saved_a[1, 0], grad_a, own)
-    out_b, back_b, more_b = step(state_b, saved_b[1, 0], grad_b, mir)
-
-    def summed(first, second):
-        both = [p + q for p, q in zip(first, second)]
-        rounded = [v.astype(BF16) for v in both]
-        return rounded[0], rounded[1], rounded[2].astype(F32), rounded[3].astype(F32)
-
-    norm, down, latent, up = reduce_grads(
-        sections, n_dp, summed(sum_a, more_a), summed(sum_b, more_b)
-    )
+    back_a, grads_a = second_back(saved_a, grad_a, own, first_a, kept_a)
+    back_b, grads_b = second_back(saved_b, grad_b, mir, first_b, kept_b)
+
+    norm, down, latent, up = reduce_grads(sections, n_dp, grads_a, grads_b)
+    state_a, state_b, norm = lax.optimization_barrier((state_a, state_b, norm))
+    out_a = forward(state_a, own)
+    out_b = forward(state_b, mir)
     return (
         out_a[None],
         out_b[None],

time: 412 us -> 398 us (0.966); the launches traced: 407 us -> 398 us
  Pallas kernels: 175 us -> 228 us
  waiting for transfers between devices: 86.3 us -> 40 us
  other arithmetic: 21.2 us -> 10.9 us
    pallas_call x1, Pallas kernels: 89.2 us -> 156 us  [reduce_grads(): pl.pallas_call(functools.partial(reduce_kernel, sections, chips), out_sha...]
    ppermute x4, waiting for transfers between devices: 86.3 us -> 40 us  [from_behind(): return lax.ppermute(block, axis, route)]
    pallas_call x1, Pallas kernels: 85.6 us -> 71.7 us  [gather(): pl.pallas_call(functools.partial(gather_kernel, sections, chips), out_sha...]
    broadcast_in_dim x2 -> x0, other arithmetic: 4.62 us -> none  [the longest x1 2.33 us: body(): back_a[None]]
    convert_element_type x10 -> x5, other arithmetic: 4.42 us -> 0.13 us  [the longest x1 0.1 us: inner(): scaled = (latent * rl * latent_gain).astype(BF16)]
    unnamed x104 -> x56, local copies, waits for them, and re-layouts: 9.38 us -> 5.67 us
  transfers between devices with their start and end apart: 4 -> 4, of which waited for: 2 -> 2; matrix products, arithmetic and copies ran while one was open for 14% -> 14% of each run, Pallas kernels for 0% -> 39%
where the time goes in v2:
time: 398 us
  Pallas kernels  228 us (57%)
  matrix products  93.2 us (23%)
  waiting for transfers between devices  40 us (10%)
  starting transfers between devices  14.4 us (4%)
  other arithmetic  10.9 us (3%)
  local copies, waits for them, and re-layouts  10.2 us (3%)
    pallas_call x1, Pallas kernels, reduce_grads(): pl.pallas_call(functools.partial(reduce_kernel, sections, chips), out_sha...  156 us
    dot_general x28, matrix products, dot(): lax.dot_general(p, q, (contract, ((), ())), preferred_element_type=F32)  93.2 us
    pallas_call x1, Pallas kernels, gather(): pl.pallas_call(functools.partial(gather_kernel, sections, chips), out_sha...  71.7 us
    ppermute x4, waiting for transfers between devices, from_behind(): return lax.ppermute(block, axis, route)  40 us
    ppermute x4, starting transfers between devices, from_behind(): return lax.ppermute(block, axis, route)  14.4 us
    reduce_sum x6, other arithmetic, inner(): r = lax.rsqrt(jnp.mean(xf * xf, axis=-1, keepdims=True) + 1e-06)  8.43 us
  transfers between devices with their start and end apart: 4, of which 2 were waited for; matrix products, arithmetic and copies ran while one was open for 14% of the time, Pallas kernels for 39%

profile of v2, /device:TPU:12, one launch (start us, length us, event | category | flops | bytes accessed | tf_op | source)
XLA Modules:
  0.0 397.6 jit_solution(18189568442221339409)
XLA Ops:
  2.0 71.7 %gather_weights.1 = (bf16[7168,256]{1,0:T(8,128)(2,1)}, bf16[256,7168]{1,0:T(8,128)(2,1)}, bf16[7168,256]{1,0:T(8,128)(2,1)}, bf16[256,7168]{1,0:T(8,128)(2,1)}, f32[64,128]{1,0:T(8,128)}) custom-call(bf16[896,256]{1,0:T(8,128)(2,1)} %bitcast.175, bf16[256,896]{1,0:T(8,128)(2,1)} %bitcast.176, f32[64,128]{1,0:T(8,128)} %fusion.128.gains), custom_call_target="tpu_custom_call" | custom-call | tf_op jit(solution)/shard_map/gather_weights/pallas_call | solution.py:205
  75.5 2.9 fusion.63
  78.4 3.0 fusion.97
  81.4 3.0 multiply_reduce_fusion.16
  85.1 4.3 %fusion.65 = (bf16[128,7168]{1,0:T(8,128)(2,1)S(1)}, bf16[128,7168]{1,0:T(8,128)(2,1)}, f32[128,7168]{1,0:T(8,128)}) fusion(f32[128]{0:T(128)S(1)} %get-tuple-element.90, f32[7168]{0:T(1024)S(1)} %slice_bitcast_fusion, bf16[2,1,128,7168]{3,2,1,0:T(8,128)(2,1)S(1)} %copy-done.4, f32[128]{0:T(128)S(1)} %broadcast_multiply_fusion.2, ...), kind=kOutput, calls=%fused_computation.95 | convolution fusion | flops 483524608 | bytes 16610816 | tf_op jit(solution)/shard_map/dot_general | solution.py:466
  89.4 3.7 collective-permute-start.1
  97.0 4.4 %fusion.62 = (bf16[128,7168]{1,0:T(8,128)(2,1)S(1)}, bf16[128,7168]{1,0:T(8,128)(2,1)}, f32[128,7168]{1,0:T(8,128)}) fusion(f32[128]{0:T(128)S(1)} %get-tuple-element.94, f32[7168]{0:T(1024)S(1)} %bitcast.179, bf16[2,1,128,7168]{3,2,1,0:T(8,128)(2,1)S(1)} %copy-done.5, f32[128]{0:T(128)S(1)} %broadcast_multiply_fusion.3, f32[128]{0:T(128)S(1)} %add_rsqrt_fusion.15, ...), kind=kOutput, calls=%fused_computation.92 | convolution fusion | flops 483524608 | bytes 16610816 | tf_op jit(solution)/shard_map/dot_general | solution.py:466
  101.3 3.5 collective-permute-start
  110.3 1.9 fusion.5
  112.3 1.9 fusion.4
  114.3 4.3 %fusion.100 = f32[7168,256]{1,0:T(8,128)} fusion(bf16[128,256]{1,0:T(8,128)(2,1)S(1)} %get-tuple-element.86, f32[7168]{0:T(1024)S(1)} %slice_bitcast_fusion, f32[128]{0:T(128)S(1)} %add_rsqrt_fusion.13, bf16[2,1,128,7168]{3,2,1,0:T(8,128)(2,1)S(1)} %copy-done.4), kind=kOutput, calls=%fused_computation.122 | convolution fusion | flops 473432064 | bytes 9269760 | tf_op jit(solution)/shard_map/dot_general | solution.py:466
  118.6 4.2 %fusion.104 = f32[7168,256]{1,0:T(8,128)} fusion(bf16[128,256]{1,0:T(8,128)(2,1)S(1)} %get-tuple-element.87, f32[7168]{0:T(1024)S(1)} %bitcast.181, f32[128]{0:T(128)S(1)} %add_rsqrt_fusion.15, bf16[2,1,128,7168]{3,2,1,0:T(8,128)(2,1)S(1)} %copy-done.5), kind=kOutput, calls=%fused_computation.124 | convolution fusion | flops 473432064 | bytes 9269760 | tf_op jit(solution)/shard_map/dot_general | solution.py:466
  122.8 4.2 %fusion.78 = f32[256,7168]{1,0:T(8,128)} fusion(bf16[1,128,7168]{2,1,0:T(8,128)(2,1)S(1)} %copy-done.9, f32[128,256]{1,0:T(8,128)S(1)} %get-tuple-element.102, f32[256]{0:T(256)S(1)} %slice_bitcast_fusion.2, f32[128]{0:T(128)S(1)} %get-tuple-element.96), kind=kOutput, calls=%fused_computation.104 | convolution fusion | flops 469860352 | bytes 9307648 | tf_op jit(solution)/shard_map/dot_general | solution.py:466
  127.0 4.1 %fusion.82 = f32[256,7168]{1,0:T(8,128)} fusion(bf16[1,128,7168]{2,1,0:T(8,128)(2,1)S(1)} %copy-done.10, f32[128,256]{1,0:T(8,128)S(1)} %get-tuple-element.100, f32[256]{0:T(256)S(1)} %bitcast.191, f32[128]{0:T(128)S(1)} %get-tuple-element.98), kind=kOutput, calls=%fused_computation.108 | convolution fusion | flops 469860352 | bytes 9307648 | tf_op jit(solution)/shard_map/dot_general | solution.py:466
  131.1 4.6 %collective-permute-done.1 = bf16[128,7168]{1,0:T(8,128)(2,1)} collective-permute-done((bf16[128,7168]{1,0:T(8,128)(2,1)}, bf16[128,7168]{1,0:T(8,128)(2,1)}, u32[]{:S(2)}, u32[]{:S(2)}) %collective-permute-start.1) | collective-permute-done | bytes 1835040 | tf_op jit(solution)/shard_map/ppermute | solution.py:462
  135.7 35.4 %collective-permute-done = bf16[128,7168]{1,0:T(8,128)(2,1)} collective-permute-done((bf16[128,7168]{1,0:T(8,128)(2,1)}, bf16[128,7168]{1,0:T(8,128)(2,1)}, u32[]{:S(2)}, u32[]{:S(2)}) %collective-permute-start) | collective-permute-done | bytes 1835040 | tf_op jit(solution)/shard_map/ppermute | solution.py:462
  171.1 2.9 multiply_reduce_fusion.6
  174.3 5.6 %fusion.24 = (f32[7168]{0:T(1024)S(1)}, f32[7168]{0:T(1024)S(1)}, bf16[1,128,7168]{2,1,0:T(8,128)(2,1)}) fusion(f32[128]{0:T(128)S(1)} %bitcast.199, bf16[2,1,128,7168]{3,2,1,0:T(8,128)(2,1)S(1)} %copy-done.4, f32[128,7168]{1,0:T(8,128)S(1)} %copy-done.17, f32[128]{0:T(128)S(1)} %add_rsqrt_fusion.13, f32[128]{0:T(128)S(1)} %broadcast_multiply_fusion, ...), kind=kOutput, calls=%fused_computation.54 | convolution fusion | flops 485345280 | bytes 14833152 | tf_op jit(solution)/shard_map/dot_general | solution.py:466
  180.6 4.3 %multiply_reduce_fusion.9 = (f32[128]{0:T(128)S(1)}, f32[128,256]{1,0:T(8,128)S(1)}) fusion(f32[128,256]{1,0:T(8,128)S(1)} %get-tuple-element.43, f32[256]{0:T(256)S(1)} %bitcast.192, bf16[128,7168]{1,0:T(8,128)(2,1)} %collective-permute-done, bf16[256,7168]{1,0:T(8,128)(2,1)} %get-tuple-element.34), kind=kOutput, calls=%fused_computation.141 | convolution fusion | flops 469860224 | bytes 5768704 | tf_op jit(solution)/shard_map/dot_general | solution.py:466
  185.2 6.9 %fusion.29 = (f32[7168]{0:T(1024)S(1)}, f32[7168]{0:T(1024)S(1)}, bf16[1,128,7168]{2,1,0:T(8,128)(2,1)}) fusion(f32[128]{0:T(128)S(1)} %bitcast.198, bf16[2,1,128,7168]{3,2,1,0:T(8,128)(2,1)S(1)} %copy-done.6, f32[128,7168]{1,0:T(8,128)} %get-tuple-element.101, f32[128]{0:T(128)S(1)} %add_rsqrt_fusion.15, f32[128]{0:T(128)S(1)} %broadcast_multiply_fusion.1, ...), kind=kOutput, calls=%fused_computation.59 | convolution fusion | flops 485345280 | bytes 14833152 | tf_op jit(solution)/shard_map/dot_general | solution.py:466
  194.8 5.3 %collective-permute-start.3 = (bf16[128,7168]{1,0:T(8,128)(2,1)}, bf16[128,7168]{1,0:T(8,128)(2,1)}, u32[]{:S(2)}, u32[]{:S(2)}) collective-permute-start(bf16[128,7168]{1,0:T(8,128)(2,1)} %fusion.5), channel_id=1, source_target_pairs={{8,0},{16,8},{24,16},{9,1},{17,9},{25,17},{10,2},{18,10},{26,18},{... | collective-permute-start | bytes 5505032 | tf_op jit(solution)/shard_map/ppermute | solution.py:462
  200.1 6.8 %fusion.3.bu = bf16[256,7168]{1,0:T(8,128)(2,1)} fusion(f32[256,7168]{1,0:T(8,128)} %fusion.78, bf16[128,256]{1,0:T(8,128)(2,1)S(1)} %get-tuple-element.50, bf16[128,7168]{1,0:T(8,128)(2,1)} %collective-permute-done.1), kind=kOutput, calls=%fused_computation.7 | convolution fusion | flops 473432064 | bytes 12910592 | tf_op jit(solution)/shard_map/dot_general | solution.py:466
  207.0 6.2 %fusion.2.bd = bf16[7168,256]{1,0:T(8,128)(2,1)} fusion(f32[7168,256]{1,0:T(8,128)} %fusion.100, bf16[128,7168]{1,0:T(8,128)(2,1)S(1)} %get-tuple-element.46, bf16[128,256]{1,0:T(8,128)(2,1)S(1)} %get-tuple-element.84), kind=kOutput, calls=%fused_computation.6 | convolution fusion | flops 473432064 | bytes 12910592 | tf_op jit(solution)/shard_map/dot_general | solution.py:466
  213.2 4.6 %fusion.1.au = bf16[256,7168]{1,0:T(8,128)(2,1)} fusion(f32[256,7168]{1,0:T(8,128)S(1)} %bitcast.172, bf16[128,256]{1,0:T(8,128)(2,1)S(1)} %get-tuple-element.44, bf16[128,7168]{1,0:T(8,128)(2,1)} %collective-permute-done), kind=kOutput, calls=%fused_computation.5 | convolution fusion | flops 473432064 | bytes 12910592 | tf_op jit(solution)/shard_map/dot_general | solution.py:466
  217.9 2.9 fusion.ad
  220.8 156.3 %reduce_grads.1 = (f32[896,256]{1,0:T(8,128)}, f32[256,896]{1,0:T(8,128)}, f32[8,128]{1,0:T(8,128)}) custom-call(bf16[7168,256]{1,0:T(8,128)(2,1)} %fusion.ad, bf16[256,7168]{1,0:T(8,128)(2,1)} %fusion.1.au, f32[8,8,128]{2,1,0:T(8,128)} %bitcast.185, bf16[7168,256]{1,0:T(8,128)(2,1)} %fusion.2.bd, bf16[256,7168]{1,0:T(8,128)(2,1)} %fusion.3.bu, ...), custom_call_target="tpu_custom_call" | custom-call | bytes 1000000 | tf_op jit(solution)/shard_map/reduce_grads/pallas_call | solution.py:439
  379.1 1.9 fusion.51
  381.0 2.4 multiply_reduce_fusion.2
  383.5 1.9 fusion.48
  385.4 2.5 multiply_reduce_fusion.3
  388.5 3.6 fusion.12
  392.2 3.6 fusion.13
  (113 shorter events, 21.4 us)
Async XLA Ops:
  73.7 4.7 %copy-start.2 = (bf16[256,7168]{1,0:T(8,128)(2,1)S(1)}, bf16[256,7168]{1,0:T(8,128)(2,1)}, u32[]{:S(2)}) copy-start(bf16[256,7168]{1,0:T(8,128)(2,1)} %get-tuple-element.37) | copy-start | bytes 11010052
  78.3 3.0 copy-start.4
  81.4 3.3 copy-start.9
  81.4 3.7 copy-start.13
  85.1 8.0 %copy-start.5 = (bf16[2,1,128,7168]{3,2,1,0:T(8,128)(2,1)S(1)}, bf16[2,1,128,7168]{3,2,1,0:T(8,128)(2,1)}, u32[]{:S(2)}) copy-start(bf16[2,1,128,7168]{3,2,1,0:T(8,128)(2,1)} %param.14) | copy-start | bytes 11010052
  85.1 8.9 %copy-start.10 = (bf16[1,128,7168]{2,1,0:T(8,128)(2,1)S(1)}, bf16[1,128,7168]{2,1,0:T(8,128)(2,1)}, u32[]{:S(2)}) copy-start(bf16[1,128,7168]{2,1,0:T(8,128)(2,1)} %param.12) | copy-start | bytes 5505028
  89.4 4.5 %copy-start = (bf16[256,7168]{1,0:T(8,128)(2,1)S(1)}, bf16[256,7168]{1,0:T(8,128)(2,1)}, u32[]{:S(2)}) copy-start(bf16[256,7168]{1,0:T(8,128)(2,1)} %get-tuple-element.34) | copy-start | bytes 11010052
  89.4 46.3 %collective-permute-start.1 = (bf16[128,7168]{1,0:T(8,128)(2,1)}, bf16[128,7168]{1,0:T(8,128)(2,1)}, u32[]{:S(2)}, u32[]{:S(2)}) collective-permute-start(bf16[128,7168]{1,0:T(8,128)(2,1)} %get-tuple-element.81), channel_id=1, source_target_pairs={{0,8},{8,16},{16,24},{1,9},{9,17},{17,25},{2,10},{10,18},{18,26},{... | collective-permute-start | bytes 5505032 | tf_op jit(solution)/shard_map/ppermute | solution.py:462
  93.9 2.0 copy-start.11
  93.9 2.0 copy-start.20
  93.9 2.0 copy-start.21
  101.3 5.1 %copy-start.7 = (bf16[128,7168]{1,0:T(8,128)(2,1)}, bf16[128,7168]{1,0:T(8,128)(2,1)S(1)}, u32[]{:S(2)}) copy-start(bf16[128,7168]{1,0:T(8,128)(2,1)S(1)} %get-tuple-element.40) | copy-start | bytes 5505028
  101.3 69.8 %collective-permute-start = (bf16[128,7168]{1,0:T(8,128)(2,1)}, bf16[128,7168]{1,0:T(8,128)(2,1)}, u32[]{:S(2)}, u32[]{:S(2)}) collective-permute-start(bf16[128,7168]{1,0:T(8,128)(2,1)} %get-tuple-element.83), channel_id=1, source_target_pairs={{8,0},{16,8},{24,16},{9,1},{17,9},{25,17},{10,2},{18,10},{26,18},{... | collective-permute-start | bytes 5505032 | tf_op jit(solution)/shard_map/ppermute | solution.py:462
  105.7 1.5 copy-start.15
  107.6 1.5 copy-start.16
  131.1 43.1 %copy-start.17 = (f32[128,7168]{1,0:T(8,128)S(1)}, f32[128,7168]{1,0:T(8,128)}, u32[]{:S(2)}) copy-start(f32[128,7168]{1,0:T(8,128)} %get-tuple-element.103) | copy-start | bytes 11010052
  180.0 5.2 %copy-start.6 = (bf16[2,1,128,7168]{3,2,1,0:T(8,128)(2,1)S(1)}, bf16[2,1,128,7168]{3,2,1,0:T(8,128)(2,1)}, u32[]{:S(2)}) copy-start(bf16[2,1,128,7168]{3,2,1,0:T(8,128)(2,1)} %param.14) | copy-start | bytes 11010052
  192.9 186.1 %collective-permute-start.2 = (bf16[128,7168]{1,0:T(8,128)(2,1)}, bf16[128,7168]{1,0:T(8,128)(2,1)}, u32[]{:S(2)}, u32[]{:S(2)}) collective-permute-start(bf16[128,7168]{1,0:T(8,128)(2,1)} %fusion.4), channel_id=1, source_target_pairs={{0,8},{8,16},{16,24},{1,9},{9,17},{17,25},{2,10},{10,18},{18,26},{... | collective-permute-start | bytes 5505032 | tf_op jit(solution)/shard_map/ppermute | solution.py:462
  194.8 184.2 %collective-permute-start.3 = (bf16[128,7168]{1,0:T(8,128)(2,1)}, bf16[128,7168]{1,0:T(8,128)(2,1)}, u32[]{:S(2)}, u32[]{:S(2)}) collective-permute-start(bf16[128,7168]{1,0:T(8,128)(2,1)} %fusion.5), channel_id=1, source_target_pairs={{8,0},{16,8},{24,16},{9,1},{17,9},{25,17},{10,2},{18,10},{26,18},{... | collective-permute-start | bytes 5505032 | tf_op jit(solution)/shard_map/ppermute | solution.py:462
  200.1 13.1 %slice-start.2 = ((s8[7340032]{0:T(1024)(128)(4,1)}), s8[4194304]{0:T(1024)(128)(4,1)S(1)}, s32[]{:S(2)}) async-start(s8[7340032]{0:T(1024)(128)(4,1)} %bitcast.171), calls=%async_computation.2 | async-start | bytes 8388608
  200.1 17.7 %slice-start = ((s8[7340032]{0:T(1024)(128)(4,1)}), s8[4194304]{0:T(1024)(128)(4,1)S(1)}, s32[]{:S(2)}) async-start(s8[7340032]{0:T(1024)(128)(4,1)} %bitcast.169), calls=%async_computation | async-start | bytes 8388608
  207.0 6.3 %slice-start.3 = ((s8[7340032]{0:T(1024)(128)(4,1)}), s8[3145728]{0:T(1024)(128)(4,1)S(1)}, s32[]{:S(2)}) async-start(s8[7340032]{0:T(1024)(128)(4,1)} %bitcast.171), calls=%async_computation.3 | async-start | bytes 6291456
  207.0 10.9 %slice-start.1 = ((s8[7340032]{0:T(1024)(128)(4,1)}), s8[3145728]{0:T(1024)(128)(4,1)S(1)}, s32[]{:S(2)}) async-start(s8[7340032]{0:T(1024)(128)(4,1)} %bitcast.169), calls=%async_computation.1 | async-start | bytes 6291456
  213.2 4.6 %copy-start.8 = (bf16[128,7168]{1,0:T(8,128)(2,1)S(1)}, bf16[128,7168]{1,0:T(8,128)(2,1)}, u32[]{:S(2)}) copy-start(bf16[128,7168]{1,0:T(8,128)(2,1)} %copy-done.7) | copy-start | bytes 5505028
  220.8 160.2 %copy-start.14 = (bf16[7168,256]{1,0:T(8,128)(2,1)S(1)}, bf16[7168,256]{1,0:T(8,128)(2,1)}, u32[]{:S(2)}) copy-start(bf16[7168,256]{1,0:T(8,128)(2,1)} %get-tuple-element.36) | copy-start | bytes 11010052
  381.0 4.4 %copy-start.12 = (bf16[7168,256]{1,0:T(8,128)(2,1)S(1)}, bf16[7168,256]{1,0:T(8,128)(2,1)}, u32[]{:S(2)}) copy-start(bf16[7168,256]{1,0:T(8,128)(2,1)} %get-tuple-element.33) | copy-start | bytes 11010052
  385.4 3.1 copy-start.3
  388.5 3.6 copy-start.1
  392.2 3.6 copy-start.19
  392.2 4.5 %copy-start.18 = (f32[256,896]{1,0:T(8,128)S(1)}, f32[256,896]{1,0:T(8,128)}, u32[]{:S(2)}) copy-start(f32[256,896]{1,0:T(8,128)} %get-tuple-element.57) | copy-start | bytes 2752516

commit v3 on v2

--- a/solution.py
+++ b/solution.py
@@ -91,6 +91,9 @@
         block = slot(mir, 1, chip, c)
         return remote(block, block, at(kind, 1, chip), at(kind + 1, 1, chip), device)
 
+    def crosses(chip):
+        return (chip > 0) & (chip < chips - 1)
+
     gain_copy = remote(gains, mgains, gain_sems.at[0], gain_sems.at[1], mirror)
     for p in range(2):
         pltpu.make_async_copy(shard[p], slot(own, p, z, c), local_sems.at[p]).start()
@@ -109,25 +112,33 @@
 
     def pass_mirror(k):
         for p in range(2):
-            for side, chip in enumerate((z - k, z + k)[: 1 if k == 0 else 2]):
+            for toward, chip in ((1, z - k), (-1, z + k))[: 1 if k == 0 else 2]:
 
                 @pl.when((chip >= 0) & (chip < chips))
                 def _():
-                    if k == 1 and p == 1:
-                        mirror_line_copy(chip, 1 if side == 0 else -1).wait_recv()
+                    if p == 0 or k == 0:
+                        mirror_copy(p, chip, slot(mir, p, chip, c)).wait_recv()
                     else:
-                        mirror_copy(p, chip, slot(mir, p, chip, c)).wait_recv()
+
+                        @pl.when(crosses(chip))
+                        def _():
+                            mirror_copy(p, chip, slot(mir, p, chip, c)).wait_recv()
+
+                        @pl.when(jnp.logical_not(crosses(chip)))
+                        def _():
+                            mirror_line_copy(chip, toward).wait_recv()
+
+                    if p == 1:
+
+                        @pl.when((chip == 0) & (z < chips - 1))
+                        def _():
+                            mirror_line_copy(chip, 1).start()
+
+                        @pl.when((chip == chips - 1) & (z > 0))
+                        def _():
+                            mirror_line_copy(chip, -1).start()
+
                     mirror_sibling_copy(p, chip).start()
-
-                if k == 0 and p == 1:
-
-                    @pl.when(z < chips - 1)
-                    def _():
-                        mirror_line_copy(z, 1).start()
-
-                    @pl.when(z > 0)
-                    def _():
-                        mirror_line_copy(z, -1).start()
 
     for k in range(1, chips):
         for p in range(2):
@@ -141,8 +152,14 @@
                 def _():
                     line_copy(p, z - k, block, 1, right).start()
 
-                if k > 1 or p == 0:
+                if p == 0:
                     mirror_copy(p, z - k, block).start()
+                else:
+
+                    @pl.when(crosses(z - k))
+                    def _():
+                        mirror_copy(p, z - k, block).start()
+
                 sibling_copy(p, z - k, block).start()
 
             @pl.when(z + k < chips)
@@ -154,8 +171,14 @@
                 def _():
                     line_copy(p, z + k, block, 2, left).start()
 
-                if k > 1 or p == 0:
+                if p == 0:
                     mirror_copy(p, z + k, block).start()
+                else:
+
+                    @pl.when(crosses(z + k))
+                    def _():
+                        mirror_copy(p, z + k, block).start()
+
                 sibling_copy(p, z + k, block).start()
 
         pass_mirror(k - 1)
@@ -170,7 +193,7 @@
                 mirror_copy(p, chip, slot(own, p, chip, c)).wait_send()
             else:
 
-                @pl.when((chip != z + 1) & (chip != z - 1))
+                @pl.when(crosses(chip) | (chip == z))
                 def _():
                     mirror_copy(p, chip, slot(own, p, chip, c)).wait_send()
 
@@ -187,11 +210,11 @@
 
     @pl.when(z < chips - 1)
     def _():
-        mirror_line_copy(z, 1).wait_send()
+        mirror_line_copy(0, 1).wait_send()
 
     @pl.when(z > 0)
     def _():
-        mirror_line_copy(z, -1).wait_send()
+        mirror_line_copy(chips - 1, -1).wait_send()
 
     gain_copy.wait()
 
@@ -513,20 +536,26 @@
     own = (norm_gain[0], owd, latent_gain[0], owu)
     mir = (mgains[:total], mwd, mgains[total : total + rank], mwu)
 
+    def normed_of(saved, gain):
+        xf = saved[:, 0].astype(F32)
+        r = lax.rsqrt(jnp.mean(xf * xf, axis=-1, keepdims=True) + 1e-06)
+        return (xf * r * gain).astype(BF16).reshape(-1, total)
+
     def first_back(saved, g, weights):
         kept = inner(saved[0, 0], *weights[:3])
         r, normed, latent, rl, scaled = kept
         d_latent, along, d_latent_gain = latent_grads(g, latent, rl, weights)
         back, d_gain = input_grads(saved[0, 0], g, r, d_latent, along, weights)
-        return back, (normed, d_latent, scaled, g, d_gain, d_latent_gain)
+        return back, (d_latent, scaled, g, d_gain, d_latent_gain)
 
     def second_back(saved, g, weights, first, kept):
         r, normed, latent, rl, scaled = kept
         d_latent, along, d_latent_gain = latent_grads(g, latent, rl, weights)
         back, d_gain = input_grads(saved[1, 0], g, r, d_latent, along, weights)
-        down = dot(first[0], first[1], ((0,), (0,))) + dot(normed, d_latent, ((0,), (0,)))
-        up = dot(first[2], first[3], ((0,), (0,))) + dot(scaled, g, ((0,), (0,)))
-        small = [(p + q).astype(BF16).astype(F32) for p, q in zip(first[4:], (d_gain, d_latent_gain))]
+        both = jnp.concatenate([first[0], d_latent])
+        down = dot(normed_of(saved, weights[0]), both, ((0,), (0,)))
+        up = dot(first[1], first[2], ((0,), (0,))) + dot(scaled, g, ((0,), (0,)))
+        small = [(p + q).astype(BF16).astype(F32) for p, q in zip(first[3:], (d_gain, d_latent_gain))]
         return back, (down.astype(BF16), up.astype(BF16), *small)
 
     back_a, first_a = first_back(saved_a, cotan_a[0], own)

time: 398 us -> 388 us (0.975)
  matrix products: 93.2 us -> 77 us
  other arithmetic: 10.9 us -> 18.3 us
    dot_general x28 -> x26, matrix products: 93.2 us -> 77 us  [dot(): lax.dot_general(p, q, (contract, ((), ())), preferred_element_type=F32)]
    convert_element_type x0 -> x2, other arithmetic: none -> 5.75 us  [normed_of(): return (xf * r * gain).astype(BF16).reshape(-1, total)]
  transfers between devices with their start and end apart: 4 -> 4, of which waited for: 2 -> 2; matrix products, arithmetic and copies ran while one was open for 14% -> 12% of each run, Pallas kernels for 39% -> 40%
where the time goes in v3:
time: 388 us; the launch traced here: 387 us
  Pallas kernels  228 us (59%)
  matrix products  77 us (20%)
  waiting for transfers between devices  37.6 us (10%)
  other arithmetic  18.3 us (5%)
  starting transfers between devices  14.3 us (4%)
  local copies, waits for them, and re-layouts  11.5 us (3%)
    pallas_call x1, Pallas kernels, reduce_grads(): pl.pallas_call(functools.partial(reduce_kernel, sections, chips), out_sha...  154 us
    dot_general x26, matrix products, dot(): lax.dot_general(p, q, (contract, ((), ())), preferred_element_type=F32)  77 us
    pallas_call x1, Pallas kernels, gather(): pl.pallas_call(functools.partial(gather_kernel, sections, chips), out_sha...  74 us
    ppermute x4, waiting for transfers between devices, from_behind(): return lax.ppermute(block, axis, route)  37.6 us
    ppermute x4, starting transfers between devices, from_behind(): return lax.ppermute(block, axis, route)  14.3 us
    reduce_sum x6, other arithmetic, inner(): r = lax.rsqrt(jnp.mean(xf * xf, axis=-1, keepdims=True) + 1e-06)  8.43 us
  transfers between devices with their start and end apart: 4, of which 2 were waited for; matrix products, arithmetic and copies ran while one was open for 12% of the time, Pallas kernels for 40%

profile of v3, /device:TPU:12, one launch (start us, length us, event | category | flops | bytes accessed | tf_op | source)
XLA Modules:
  0.0 387.4 jit_solution(13569669593763444455)
XLA Ops:
  2.0 74.0 %gather_weights.1 = (bf16[7168,256]{1,0:T(8,128)(2,1)}, bf16[256,7168]{1,0:T(8,128)(2,1)}, bf16[7168,256]{1,0:T(8,128)(2,1)}, bf16[256,7168]{1,0:T(8,128)(2,1)}, f32[64,128]{1,0:T(8,128)}) custom-call(bf16[896,256]{1,0:T(8,128)(2,1)} %bitcast.187, bf16[256,896]{1,0:T(8,128)(2,1)} %bitcast.188, f32[64,128]{1,0:T(8,128)} %fusion.140.gains), custom_call_target="tpu_custom_call" | custom-call | tf_op jit(solution)/shard_map/gather_weights/pallas_call | solution.py:228
  77.8 2.9 fusion.65
  80.7 3.0 fusion.111
  83.7 3.0 multiply_reduce_fusion.18
  87.4 4.6 %fusion.67 = (bf16[128,7168]{1,0:T(8,128)(2,1)}, bf16[128,7168]{1,0:T(8,128)(2,1)}, f32[128,7168]{1,0:T(8,128)}) fusion(f32[128]{0:T(128)S(1)} %get-tuple-element.86, f32[7168]{0:T(1024)S(1)} %slice_bitcast_fusion, bf16[2,1,128,7168]{3,2,1,0:T(8,128)(2,1)S(1)} %copy-done.5, f32[128]{0:T(128)S(1)} %broadcast_multiply_fusion.2, ...), kind=kOutput, calls=%fused_computation.101 | convolution fusion | flops 483524608 | bytes 16610816 | tf_op jit(solution)/shard_map/dot_general | solution.py:489
  92.0 3.6 collective-permute-start.1
  99.5 4.7 %fusion.64 = (bf16[128,7168]{1,0:T(8,128)(2,1)}, bf16[128,7168]{1,0:T(8,128)(2,1)}, f32[128,7168]{1,0:T(8,128)}) fusion(f32[128]{0:T(128)S(1)} %get-tuple-element.90, f32[7168]{0:T(1024)S(1)} %bitcast.191, bf16[2,1,128,7168]{3,2,1,0:T(8,128)(2,1)S(1)} %copy-done.6, f32[128]{0:T(128)S(1)} %broadcast_multiply_fusion.3, f32[128]{0:T(128)S(1)} %add_rsqrt_fusion.15, ...), kind=kOutput, calls=%fused_computation.98 | convolution fusion | flops 483524608 | bytes 16610816 | tf_op jit(solution)/shard_map/dot_general | solution.py:489
  104.1 3.6 collective-permute-start
  107.7 4.2 %fusion.85 = f32[256,7168]{1,0:T(8,128)} fusion(bf16[1,128,7168]{2,1,0:T(8,128)(2,1)S(1)} %copy-done.8, f32[128,256]{1,0:T(8,128)S(1)} %get-tuple-element.98, f32[256]{0:T(256)S(1)} %slice_bitcast_fusion.2, f32[128]{0:T(128)S(1)} %get-tuple-element.92), kind=kOutput, calls=%fused_computation.113 | convolution fusion | flops 469860352 | bytes 9307648 | tf_op jit(solution)/shard_map/dot_general | solution.py:489
  112.8 4.2 %fusion.90 = f32[256,7168]{1,0:T(8,128)} fusion(bf16[1,128,7168]{2,1,0:T(8,128)(2,1)S(1)} %copy-done.9, f32[128,256]{1,0:T(8,128)S(1)} %get-tuple-element.96, f32[256]{0:T(256)S(1)} %bitcast.201, f32[128]{0:T(128)S(1)} %get-tuple-element.94), kind=kOutput, calls=%fused_computation.118 | convolution fusion | flops 469860352 | bytes 9307648 | tf_op jit(solution)/shard_map/dot_general | solution.py:489
  123.9 2.9 fusion.13
  126.8 1.9 fusion.3
  128.8 1.9 fusion.2
  130.8 2.9 fusion.15
  133.7 4.5 %collective-permute-done.1 = bf16[128,7168]{1,0:T(8,128)(2,1)S(1)} collective-permute-done((bf16[128,7168]{1,0:T(8,128)(2,1)}, bf16[128,7168]{1,0:T(8,128)(2,1)S(1)}, u32[]{:S(2)}, u32[]{:S(2)}) %collective-permute-start.1) | collective-permute-done | bytes 1835040 | tf_op jit(solution)/shard_map/ppermute | solution.py:485
  138.2 33.0 %collective-permute-done = bf16[128,7168]{1,0:T(8,128)(2,1)S(1)} collective-permute-done((bf16[128,7168]{1,0:T(8,128)(2,1)}, bf16[128,7168]{1,0:T(8,128)(2,1)S(1)}, u32[]{:S(2)}, u32[]{:S(2)}) %collective-permute-start) | collective-permute-done | bytes 1835040 | tf_op jit(solution)/shard_map/ppermute | solution.py:485
  172.9 4.3 %fusion.26 = (f32[7168]{0:T(1024)S(1)}, f32[7168]{0:T(1024)S(1)}, bf16[1,128,7168]{2,1,0:T(8,128)(2,1)}) fusion(f32[128]{0:T(128)S(1)} %bitcast.211, bf16[2,1,128,7168]{3,2,1,0:T(8,128)(2,1)S(1)} %copy-done.5, f32[128,7168]{1,0:T(8,128)S(1)} %copy-done.22, f32[128]{0:T(128)S(1)} %add_rsqrt_fusion.13, f32[128]{0:T(128)S(1)} %broadcast_multiply_fusion, ...), kind=kOutput, calls=%fused_computation.60 | convolution fusion | flops 485345280 | bytes 14833152 | tf_op jit(solution)/shard_map/dot_general | solution.py:489
  178.0 5.2 %convolution_convert_fusion.bd = bf16[7168,256]{1,0:T(8,128)(2,1)} fusion(bf16[256,7168]{1,0:T(8,128)(2,1)} %fusion.13, bf16[128,256]{1,0:T(8,128)(2,1)S(1)} %get-tuple-element.80, bf16[128,256]{1,0:T(8,128)(2,1)S(1)} %get-tuple-element.82), kind=kOutput, calls=%fused_computation.4 | convolution fusion | flops 941621248 | bytes 7471104 | tf_op jit(solution)/shard_map/dot_general | solution.py:489
  183.1 1.4 multiply_reduce_fusion.11
  185.3 5.6 %fusion.31 = (f32[7168]{0:T(1024)S(1)}, f32[7168]{0:T(1024)S(1)}, bf16[1,128,7168]{2,1,0:T(8,128)(2,1)}) fusion(f32[128]{0:T(128)S(1)} %bitcast.210, bf16[2,1,128,7168]{3,2,1,0:T(8,128)(2,1)S(1)} %copy-done.7, f32[128,7168]{1,0:T(8,128)} %get-tuple-element.97, f32[128]{0:T(128)S(1)} %add_rsqrt_fusion.15, f32[128]{0:T(128)S(1)} %broadcast_multiply_fusion.1, ...), kind=kOutput, calls=%fused_computation.65 | convolution fusion | flops 485345280 | bytes 14833152 | tf_op jit(solution)/shard_map/dot_general | solution.py:489
  191.7 1.9 collective-permute-start.2
  193.6 5.2 %collective-permute-start.3 = (bf16[128,7168]{1,0:T(8,128)(2,1)}, bf16[128,7168]{1,0:T(8,128)(2,1)}, u32[]{:S(2)}, u32[]{:S(2)}) collective-permute-start(bf16[128,7168]{1,0:T(8,128)(2,1)} %fusion.3), channel_id=1, source_target_pairs={{8,0},{16,8},{24,16},{9,1},{17,9},{25,17},{10,2},{18,10},{26,18},{... | collective-permute-start | bytes 5505032 | tf_op jit(solution)/shard_map/ppermute | solution.py:485
  198.8 5.1 %convolution_convert_fusion.1.ad = bf16[7168,256]{1,0:T(8,128)(2,1)} fusion(bf16[256,7168]{1,0:T(8,128)(2,1)} %fusion.15, bf16[128,256]{1,0:T(8,128)(2,1)S(1)} %get-tuple-element.81, bf16[128,256]{1,0:T(8,128)(2,1)S(1)} %get-tuple-element.83), kind=kOutput, calls=%fused_computation.5 | convolution fusion | flops 941621248 | bytes 7471104 | tf_op jit(solution)/shard_map/dot_general | solution.py:489
  204.0 6.2 %fusion.1.bu = bf16[256,7168]{1,0:T(8,128)(2,1)} fusion(f32[256,7168]{1,0:T(8,128)} %fusion.85, bf16[128,256]{1,0:T(8,128)(2,1)S(1)} %get-tuple-element.46, bf16[128,7168]{1,0:T(8,128)(2,1)S(1)} %collective-permute-done.1), kind=kOutput, calls=%fused_computation.3 | convolution fusion | flops 473432064 | bytes 12910592 | tf_op jit(solution)/shard_map/dot_general | solution.py:489
  210.2 2.9 fusion.au
  213.1 153.8 %reduce_grads.1 = (f32[896,256]{1,0:T(8,128)}, f32[256,896]{1,0:T(8,128)}, f32[8,128]{1,0:T(8,128)}) custom-call(bf16[7168,256]{1,0:T(8,128)(2,1)} %convolution_convert_fusion.1.ad, bf16[256,7168]{1,0:T(8,128)(2,1)} %fusion.au, f32[8,8,128]{2,1,0:T(8,128)} %bitcast.197, bf16[7168,256]{1,0:T(8,128)(2,1)} %convolution_convert_fusion.bd, ...), custom_call_target="tpu_custom_call" | custom-call | bytes 1000000 | tf_op jit(solution)/shard_map/reduce_grads/pallas_call | solution.py:462
  368.8 1.9 fusion.53
  370.8 2.4 multiply_reduce_fusion.4
  373.2 1.9 fusion.50
  375.2 2.5 multiply_reduce_fusion.5
  378.3 3.6 fusion.10
  381.9 3.6 fusion.11
  (122 shorter events, 23.8 us)
Async XLA Ops:
  76.0 4.7 %copy-start.3 = (bf16[256,7168]{1,0:T(8,128)(2,1)S(1)}, bf16[256,7168]{1,0:T(8,128)(2,1)}, u32[]{:S(2)}) copy-start(bf16[256,7168]{1,0:T(8,128)(2,1)} %get-tuple-element.35) | copy-start | bytes 11010052
  80.6 3.0 copy-start.5
  83.7 3.2 copy-start.8
  83.7 3.7 copy-start.13
  87.4 8.2 %copy-start.6 = (bf16[2,1,128,7168]{3,2,1,0:T(8,128)(2,1)S(1)}, bf16[2,1,128,7168]{3,2,1,0:T(8,128)(2,1)}, u32[]{:S(2)}) copy-start(bf16[2,1,128,7168]{3,2,1,0:T(8,128)(2,1)} %param.14) | copy-start | bytes 11010052
  87.4 9.1 %copy-start.9 = (bf16[1,128,7168]{2,1,0:T(8,128)(2,1)S(1)}, bf16[1,128,7168]{2,1,0:T(8,128)(2,1)}, u32[]{:S(2)}) copy-start(bf16[1,128,7168]{2,1,0:T(8,128)(2,1)} %param.12) | copy-start | bytes 5505028
  92.0 4.4 %copy-start = (bf16[256,7168]{1,0:T(8,128)(2,1)S(1)}, bf16[256,7168]{1,0:T(8,128)(2,1)}, u32[]{:S(2)}) copy-start(bf16[256,7168]{1,0:T(8,128)(2,1)} %get-tuple-element.32) | copy-start | bytes 11010052
  92.0 46.2 %collective-permute-start.1 = (bf16[128,7168]{1,0:T(8,128)(2,1)}, bf16[128,7168]{1,0:T(8,128)(2,1)S(1)}, u32[]{:S(2)}, u32[]{:S(2)}) collective-permute-start(bf16[128,7168]{1,0:T(8,128)(2,1)} %get-tuple-element.77), channel_id=1, source_target_pairs={{0,8},{8,16},{16,24},{1,9},{9,17},{17,25},{2,10},{10,18},{18,26},{... | collective-permute-start | bytes 5505032 | tf_op jit(solution)/shard_map/ppermute | solution.py:485
  96.4 2.0 copy-start.10
  96.4 2.0 copy-start.25
  96.4 2.0 copy-start.26
  104.1 67.1 %collective-permute-start = (bf16[128,7168]{1,0:T(8,128)(2,1)}, bf16[128,7168]{1,0:T(8,128)(2,1)S(1)}, u32[]{:S(2)}, u32[]{:S(2)}) collective-permute-start(bf16[128,7168]{1,0:T(8,128)(2,1)} %get-tuple-element.79), channel_id=1, source_target_pairs={{8,0},{16,8},{24,16},{9,1},{17,9},{25,17},{10,2},{18,10},{26,18},{... | collective-permute-start | bytes 5505032 | tf_op jit(solution)/shard_map/ppermute | solution.py:485
  117.0 1.5 copy-start.20
  117.8 1.6 copy-start.21
  119.2 1.6 copy-start.18
  121.2 1.5 copy-start.19
  133.7 39.2 %copy-start.22 = (f32[128,7168]{1,0:T(8,128)S(1)}, f32[128,7168]{1,0:T(8,128)}, u32[]{:S(2)}) copy-start(f32[128,7168]{1,0:T(8,128)} %get-tuple-element.99) | copy-start | bytes 11010052
  178.0 5.2 %copy-start.1 = (bf16[256,7168]{1,0:T(8,128)(2,1)S(1)}, bf16[256,7168]{1,0:T(8,128)(2,1)}, u32[]{:S(2)}) copy-start(bf16[256,7168]{1,0:T(8,128)(2,1)} %get-tuple-element.32) | copy-start | bytes 11010052
  178.0 5.2 %copy-start.16 = (bf16[128,7168]{1,0:T(8,128)(2,1)S(1)}, bf16[128,7168]{1,0:T(8,128)(2,1)}, u32[]{:S(2)}) copy-start(bf16[128,7168]{1,0:T(8,128)(2,1)} %copy-done.15) | copy-start | bytes 5505028
  178.0 6.8 %copy-start.11 = (bf16[7168,256]{1,0:T(8,128)(2,1)S(1)}, bf16[7168,256]{1,0:T(8,128)(2,1)}, u32[]{:S(2)}) copy-start(bf16[7168,256]{1,0:T(8,128)(2,1)} %get-tuple-element.31) | copy-start | bytes 11010052
  183.1 2.2 copy-start.7
  191.7 177.1 %collective-permute-start.2 = (bf16[128,7168]{1,0:T(8,128)(2,1)}, bf16[128,7168]{1,0:T(8,128)(2,1)}, u32[]{:S(2)}, u32[]{:S(2)}) collective-permute-start(bf16[128,7168]{1,0:T(8,128)(2,1)} %fusion.2), channel_id=1, source_target_pairs={{0,8},{8,16},{16,24},{1,9},{9,17},{17,25},{2,10},{10,18},{18,26},{... | collective-permute-start | bytes 5505032 | tf_op jit(solution)/shard_map/ppermute | solution.py:485
  193.6 175.2 %collective-permute-start.3 = (bf16[128,7168]{1,0:T(8,128)(2,1)}, bf16[128,7168]{1,0:T(8,128)(2,1)}, u32[]{:S(2)}, u32[]{:S(2)}) collective-permute-start(bf16[128,7168]{1,0:T(8,128)(2,1)} %fusion.3), channel_id=1, source_target_pairs={{8,0},{16,8},{24,16},{9,1},{17,9},{25,17},{10,2},{18,10},{26,18},{... | collective-permute-start | bytes 5505032 | tf_op jit(solution)/shard_map/ppermute | solution.py:485
  198.8 11.3 %slice-start = ((s8[7340032]{0:T(1024)(128)(4,1)}), s8[4194304]{0:T(1024)(128)(4,1)S(1)}, s32[]{:S(2)}) async-start(s8[7340032]{0:T(1024)(128)(4,1)} %bitcast.183), calls=%async_computation | async-start | bytes 8388608
  204.0 6.2 %slice-start.1 = ((s8[7340032]{0:T(1024)(128)(4,1)}), s8[3145728]{0:T(1024)(128)(4,1)S(1)}, s32[]{:S(2)}) async-start(s8[7340032]{0:T(1024)(128)(4,1)} %bitcast.183), calls=%async_computation.1 | async-start | bytes 6291456
  204.0 6.2 %copy-start.17 = (bf16[128,7168]{1,0:T(8,128)(2,1)S(1)}, bf16[128,7168]{1,0:T(8,128)(2,1)}, u32[]{:S(2)}) copy-start(bf16[128,7168]{1,0:T(8,128)(2,1)} %copy-done.15) | copy-start | bytes 5505028
  213.1 157.6 %copy-start.14 = (bf16[7168,256]{1,0:T(8,128)(2,1)S(1)}, bf16[7168,256]{1,0:T(8,128)(2,1)}, u32[]{:S(2)}) copy-start(bf16[7168,256]{1,0:T(8,128)(2,1)} %get-tuple-element.34) | copy-start | bytes 11010052
  370.8 4.4 %copy-start.12 = (bf16[7168,256]{1,0:T(8,128)(2,1)S(1)}, bf16[7168,256]{1,0:T(8,128)(2,1)}, u32[]{:S(2)}) copy-start(bf16[7168,256]{1,0:T(8,128)(2,1)} %get-tuple-element.31) | copy-start | bytes 11010052
  375.2 3.1 copy-start.4
  378.3 3.6 copy-start.2
  381.9 3.6 copy-start.24
  381.9 4.5 %copy-start.23 = (f32[256,896]{1,0:T(8,128)S(1)}, f32[256,896]{1,0:T(8,128)}, u32[]{:S(2)}) copy-start(f32[256,896]{1,0:T(8,128)} %get-tuple-element.53) | copy-start | bytes 2752516
  (1 other events, 1.4 us)
